TPU v7x, 256 devices: a whole 4x4x8 slice. The times are simulated.
256 devices in a mesh: key: 8 (over x, core), hid: 32 (over z, y).
Axes of the slice: x: 4, y: 4, z: 8, core: 2. Of those that a mesh axis runs over, the one named last changes fastest.
Arguments:
- queries: bfloat16 [2048, 6144], P(('key', 'hid')), may hold values from -256 to 256
- cache_keys: bfloat16 [6144, 1024], P('key'), may hold values from -8 to 8
- cache_values: bfloat16 [6144, 1024], P('key'), may hold values from -6 to 6
- response_kv: bfloat16 [2048, 2048], P(('key', 'hid')), may hold values from -7 to 7
- segments: int32 [2048], replicated, may hold values from 0 to 3, never falling along the last dimension, each value on 1 to 1024 neighbouring positions
- residual: bfloat16 [2048, 6144], P(('key', 'hid')), may hold values from -6 to 6
- out_weight: bfloat16 [6144, 6144], P('hid', 'key'), may hold values from -1.5 to 1.5
- norm_gain: float32 [6144], replicated, may hold values from 0.5 to 1.5
- up_weight: bfloat16 [6144, 12288], P(None, 'hid'), may hold values from -0.078125 to 0.078125
- down_weight: bfloat16 [12288, 6144], P('hid'), may hold values from -0.0546875 to 0.0546875
Outputs:
- layer_out: bfloat16 [2048, 6144], P(('key', 'hid'))
All inputs are finite; a program needn't handle non-finite values.
Results may differ from a plain program's by a relative error of at most 0.025.
Values may be sent and summed in bfloat16 or wider, within the bound.
A program may use at most 128 MiB of HBM per device.

v0:
```python
import math

import jax
import jax.numpy as jnp
from jax import lax
from jax.sharding import PartitionSpec as P

HEADS = 48
KV_HEADS = 8
HEAD = 128
GROUP = 6


def combined_all(part, axis, combine):
    gathered = jax.tree.map(lambda a: lax.all_gather(a, axis), part)

    def take(source):
        return jax.tree.map(lambda a: lax.dynamic_index_in_dim(a, source, 0, False), gathered)

    return lax.fori_loop(
        1, lax.axis_size(axis), lambda source, state: combine(state, take(source)), take(0)
    )


def layer_norm(hidden, gain):
    wide = hidden.astype(jnp.float32)
    mean = jnp.mean(wide, axis=-1, keepdims=True)
    centred = wide - mean
    var = jnp.mean(centred * centred, axis=-1, keepdims=True)
    return (centred * lax.rsqrt(var + 1e-05) * gain).astype(jnp.bfloat16)


def join(first, second):
    top = jnp.maximum(first[0], second[0])
    left = jnp.exp(first[0] - top)
    right = jnp.exp(second[0] - top)
    return (
        top,
        first[1] * left + second[1] * right,
        first[2] * left[..., None] + second[2] * right[..., None],
    )


def on_device(
    queries,
    cache_keys,
    cache_values,
    response_kv,
    segments,
    residual,
    out_weight,
    norm_gain,
    up_weight,
    down_weight,
):
    n_hid = lax.axis_size("hid")
    key_idx = lax.axis_index("key")
    hid_idx = lax.axis_index("hid")
    tok = queries.shape[0]
    width = cache_keys.shape[1]
    ctx_dev = cache_keys.shape[0]
    q_all, wo_full = (
        lax.all_gather(queries, "key", axis=0, tiled=True),
        lax.all_gather(out_weight, "key", axis=1, tiled=True),
    )
    group_kv = lax.all_gather(response_kv, "hid", axis=0, tiled=True)
    group_rows = group_kv.shape[0]
    keys = jnp.concatenate([cache_keys, group_kv[:, :width]], 0).reshape(-1, KV_HEADS, HEAD)
    values = (
        jnp.concatenate([cache_values, group_kv[:, width:]], 0)
        .astype(jnp.float32)
        .reshape(-1, KV_HEADS, HEAD)
    )
    key_rows = jnp.concatenate(
        [
            jnp.full((ctx_dev,), -1, jnp.int32),
            key_idx * group_rows + jnp.arange(group_rows, dtype=jnp.int32),
        ]
    )
    own_seg = lax.dynamic_slice_in_dim(segments, key_idx * group_rows, group_rows)
    key_seg = jnp.concatenate([jnp.full((ctx_dev,), -1, jnp.int32), own_seg])
    count = q_all.shape[0]
    slot = jnp.arange(count, dtype=jnp.int32)
    q_rows = (slot // tok * n_hid + hid_idx) * tok + slot % tok
    q_seg = jnp.take(segments, q_rows)
    scale = 1.0 / math.sqrt(HEAD)
    grouped = q_all.reshape(count, KV_HEADS, GROUP, HEAD)
    score = jnp.einsum("bgjd,ngd->bgjn", grouped, keys, preferred_element_type=jnp.float32) * scale
    seen = (key_rows[None, :] < 0) | (key_seg[None, :] == q_seg[:, None]) & (
        key_rows[None, :] <= q_rows[:, None]
    )
    score = jnp.where(seen[:, None, None, :], score, -jnp.inf)
    top = jnp.max(score, axis=-1)
    weight = jnp.exp(score - top[..., None])
    summed = jnp.sum(weight, axis=-1)
    mixed = jnp.einsum("bgjn,ngd->bgjd", weight, values)
    top = top.reshape(count, HEADS)
    summed = summed.reshape(count, HEADS)
    mixed = mixed.reshape(count, HEADS, HEAD)
    top_all, sum_all, mix_all = combined_all((top, summed, mixed), "key", join)
    own = (
        lax.dynamic_slice_in_dim(top_all, key_idx * tok, tok, 0),
        lax.dynamic_slice_in_dim(sum_all, key_idx * tok, tok, 0),
        lax.dynamic_slice_in_dim(mix_all, key_idx * tok, tok, 0),
    )
    attn = (own[2] / own[1][..., None]).reshape(tok, HEADS * HEAD).astype(jnp.bfloat16)
    attn_cols = lax.all_to_all(attn, "hid", split_axis=1, concat_axis=0, tiled=True)
    block = attn_cols
    proj = lax.psum_scatter(
        jnp.dot(block, wo_full, preferred_element_type=jnp.float32).astype(jnp.bfloat16),
        "hid",
        scatter_dimension=0,
        tiled=True,
    ).astype(jnp.float32)
    mid = (residual.astype(jnp.float32) + proj).astype(jnp.bfloat16)
    normed = layer_norm(mid, norm_gain)
    up = jnp.dot(
        lax.all_gather(normed, "hid", axis=0, tiled=True),
        up_weight,
        preferred_element_type=jnp.float32,
    )
    active = jnp.square(jnp.maximum(up, 0.0)).astype(jnp.bfloat16)
    block = active
    down = lax.psum_scatter(
        jnp.dot(block, down_weight, preferred_element_type=jnp.float32).astype(jnp.bfloat16),
        "hid",
        scatter_dimension=0,
        tiled=True,
    ).astype(jnp.float32)
    return (mid.astype(jnp.float32) + down).astype(jnp.bfloat16)


def solution(mesh):
    return jax.shard_map(
        on_device,
        mesh=mesh,
        in_specs=(
            P(("key", "hid"), None),
            P("key", None),
            P("key", None),
            P(("key", "hid"), None),
            P(),
            P(("key", "hid"), None),
            P("hid", "key"),
            P(),
            P(None, "hid"),
            P("hid", None),
        ),
        out_specs=P(("key", "hid"), None),
        check_vma=False,
    )
```

profile of v0, /device:TPU:2, one launch (start us, length us, event | category | flops | bytes accessed | tf_op | source)
XLA Modules:
  0.0 750.6 jit_solution(4028817050251032443)
XLA Ops:
  6.5 0.7 all-gather.5.cloned.1.call-update
  7.3 0.8 dynamic_slice.50
  8.1 1.5 gather_fusion
  9.6 1.7 copy.26
  11.3 13.5 %all_gather.22 = bf16[64,6144]{1,0:T(8,128)(2,1)S(1)} all-gather(bf16[8,6144]{1,0:T(8,128)(2,1)S(1)} %copy-done.4), channel_id=1, replica_groups=mesh['key'=8,'hid'=32] {'key'}, dimensions={0}, use_global_device_ids=true | all-gather | bytes 884736 | tf_op jit(solution)/shard_map/all_gather | solution.py:63
  24.9 2.0 reshape.178
  26.9 1.7 copy.30
  28.6 0.1 and_or_fusion
  28.8 60.4 %all-gather.5.cloned.1.call-done = bf16[256,2048]{1,0:T(8,128)(2,1)} async-done(((bf16[8,2048]{1,0:T(8,128)(2,1)}), bf16[256,2048]{1,0:T(8,128)(2,1)}) %all-gather.5.cloned.1.call-update) | async-done | bytes 1048592 | tf_op jit(solution)/shard_map/all_gather | solution.py:66
  89.1 2.3 fusion.35
  91.4 2.0 copy.46
  93.4 2.0 copy.47
  95.5 1.4 pad_maximum_fusion
  96.9 1.6 pad_maximum_fusion.1
  98.5 2.6 fusion.5
  101.1 2.8 fusion.3
  103.9 1.6 copy-done
  105.6 2.1 copy.32
  107.7 0.7 all-gather.9.cloned.1.call-update
  108.4 6.5 fusion.4
  115.0 13.0 %all_gather.23 = f32[8,64,48]{1,2,0:T(8,128)S(1)} all-gather(f32[1,64,48]{1,2,0:T(8,128)S(1)} %all_gather_reshape.9), channel_id=1, replica_groups=mesh['key'=8,'hid'=32] {'key'}, dimensions={0}, use_global_device_ids=true | all-gather | bytes 110592 | tf_op jit(solution)/shard_map/all_gather | solution.py:15
  128.0 0.1 copy.33
  128.1 13.2 %all_gather.24 = f32[8,64,48]{1,2,0:T(8,128)S(1)} all-gather(f32[1,64,48]{1,2,0:T(8,128)S(1)} %all_gather_reshape.10), channel_id=1, replica_groups=mesh['key'=8,'hid'=32] {'key'}, dimensions={0}, use_global_device_ids=true | all-gather | bytes 110592 | tf_op jit(solution)/shard_map/all_gather | solution.py:15
  141.3 0.1 copy.34
  141.4 34.4 %all-gather.7.cloned.1.call-done = f32[8,64,48,128]{3,2,1,0:T(8,128)} async-done(((f32[1,64,48,128]{3,2,1,0:T(8,128)}), f32[8,64,48,128]{3,2,1,0:T(8,128)}) %all-gather.7.cloned.1.call-update) | async-done | bytes 12582928 | tf_op jit(solution)/shard_map/all_gather | solution.py:15
  175.8 1.5 slice_bitcast_fusion
  177.3 17.5 %while.19 = (s32[]{:T(128)}, f32[64,48]{1,0:T(8,128)S(1)}, f32[64,48]{1,0:T(8,128)S(1)}, f32[64,48,128]{2,1,0:T(8,128)S(1)}, f32[8,64,48]{1,2,0:T(8,128)S(1)}, /...) while((s32[]{:T(128)}, f32[64,48]{1,0:T(8,128)S(1)}, ...), condition=%wide.region_3.4_spmd, body=%wide.region_2.3_spmd.sunk | while | flops 1198085 | bytes 4939927 | solution.py:20
  177.5 2.2 fusion.45
  180.0 2.2 fusion.45
  182.5 2.2 fusion.45
  185.0 2.2 fusion.45
  187.5 2.2 fusion.45
  190.0 2.3 fusion.45
  192.5 2.2 fusion.45
  194.8 0.1 divide_convert_fusion
  195.0 0.1 convert_element_type.41
  195.1 0.7 copy.37
  195.8 9.7 %all-to-all-start = ((bf16[8,32,192]{2,0,1:T(8,128)(2,1)}), bf16[8,32,192]{2,0,1:T(8,128)(2,1)S(1)}, u32[]{:S(2)}, u32[]{:S(2)}) async-start(bf16[8,32,192]{2,0,1:T(8,128)(2,1)} %copy.37), calls=%async_computation | async-start | bytes 262144 | tf_op jit(solution)/shard_map/all_to_all | solution.py:107
  205.6 10.8 %all-to-all-done = bf16[8,32,192]{2,0,1:T(8,128)(2,1)S(1)} async-done(((bf16[8,32,192]{2,0,1:T(8,128)(2,1)}), bf16[8,32,192]{2,0,1:T(8,128)(2,1)S(1)}, u32[]{:S(2)}, u32[]{:S(2)}) %all-to-all-start) | async-done | bytes 98336 | tf_op jit(solution)/shard_map/all_to_all | solution.py:107
  216.4 4.3 convolution_convert_fusion.1
  220.8 214.1 %reduce-scatter.3.cloned.1.call-done = bf16[8,6144]{1,0:T(8,128)(2,1)} async-done(((bf16[256,6144]{1,0:T(8,128)(2,1)}), bf16[8,6144]{1,0:T(8,128)(2,1)}) %reduce-scatter.3.cloned.1.call-update) | async-done | bytes 98320 | tf_op jit(solution)/shard_map/reduce_scatter | solution.py:109
  434.9 1.1 convert_reduce_fusion
  436.0 0.2 fusion.16
  436.3 0.7 fusion.18
  437.1 78.8 %all-gather.11.cloned.1.call-done = bf16[256,6144]{1,0:T(8,128)(2,1)} async-done(((bf16[8,6144]{1,0:T(8,128)(2,1)}), bf16[256,6144]{1,0:T(8,128)(2,1)}) %all-gather.11.cloned.1.call-update) | async-done | bytes 3145744 | tf_op jit(solution)/shard_map/all_gather | solution.py:118
  515.8 9.9 %convolution_convert_fusion = bf16[256,6144]{1,0:T(8,128)(2,1)} fusion(bf16[384,6144]{1,0:T(8,128)(2,1)} %param.21, bf16[256,6144]{1,0:T(8,128)(2,1)} %all-gather.11.cloned.1.call-done, bf16[6144,384]{1,0:T(8,128)(2,1)} %param.20), kind=kOutput, calls=%fused_computation.16 | convolution fusion | flops 2417786880 | bytes 15728640 | tf_op jit(solution)/shard_map/dot_general | solution.py:125
  525.7 216.5 %reduce-scatter.5.cloned.1.call-done = bf16[8,6144]{1,0:T(8,128)(2,1)} async-done(((bf16[256,6144]{1,0:T(8,128)(2,1)}), bf16[8,6144]{1,0:T(8,128)(2,1)}) %reduce-scatter.5.cloned.1.call-update) | async-done | bytes 98320 | tf_op jit(solution)/shard_map/reduce_scatter | solution.py:124
  742.2 1.6 fusion.19
  (66 shorter events, 1.9 us)
Async XLA Ops:
  6.5 4.8 copy-start.4
  6.5 82.6 %all-gather.5.cloned.1.call-start = ((), (), s32[]{:S(2)}) async-start(), calls=%async_computation.3 | async-start | bytes 1081344 | tf_op jit(solution)/shard_map/all_gather | solution.py:66
  7.3 168.5 %all-gather.7.cloned.1.call-start = ((), (), s32[]{:S(2)}) async-start(), calls=%async_computation.4 | async-start | bytes 14155776 | tf_op jit(solution)/shard_map/all_gather | solution.py:15
  95.5 1.4 copy-start.3
  96.9 1.6 copy-start.1
  98.5 2.6 copy-start.2
  101.1 4.5 copy-start
  107.7 98.0 %all-gather.9.cloned.1.call-start = ((), (), s32[]{:S(2)}) async-start(), calls=%async_computation.5 | async-start | bytes 2654208 | tf_op jit(solution)/shard_map/all_gather | solution.py:64
  195.8 20.6 %all-to-all-start = ((bf16[8,32,192]{2,0,1:T(8,128)(2,1)}), bf16[8,32,192]{2,0,1:T(8,128)(2,1)S(1)}, u32[]{:S(2)}, u32[]{:S(2)}) async-start(bf16[8,32,192]{2,0,1:T(8,128)(2,1)} %copy.37), calls=%async_computation | async-start | bytes 262144 | tf_op jit(solution)/shard_map/all_to_all | solution.py:107
  205.5 229.4 %copy-start.5 = (bf16[8,6144]{1,0:T(8,128)(2,1)S(1)}, bf16[8,6144]{1,0:T(8,128)(2,1)}, u32[]{:S(2)}) copy-start(bf16[8,6144]{1,0:T(8,128)(2,1)} %param.17) | copy-start | bytes 294916
  205.6 229.4 %reduce-scatter.3.cloned.1.call-start = ((), (), s32[]{:S(2)}) async-start(), calls=%async_computation.6 | async-start | bytes 3244032 | tf_op jit(solution)/shard_map/reduce_scatter | solution.py:109
  220.7 215.5 %copy-start.6 = (f32[6144]{0:T(1024)S(1)}, f32[6144]{0:T(1024)}, u32[]{:S(2)}) copy-start(f32[6144]{0:T(1024)} %param.19) | copy-start | bytes 73732
  220.8 295.1 %all-gather.11.cloned.1.call-start = ((), (), s32[]{:S(2)}) async-start(), calls=%async_computation.7 | async-start | bytes 3244032 | tf_op jit(solution)/shard_map/all_gather | solution.py:118
  437.0 305.2 %reduce-scatter.5.cloned.1.call-start = ((), (), s32[]{:S(2)}) async-start(), calls=%async_computation.8 | async-start | bytes 3244032 | tf_op jit(solution)/shard_map/reduce_scatter | solution.py:124
Sparse Core Ops, SparseCore 0:
  9.9 79.1 all-gather.4
  107.8 67.9 all-gather.6
  177.6 27.7 all-gather.8
  220.9 214.0 reduce-scatter.2
  437.7 78.1 all-gather.10
  525.9 216.3 reduce-scatter.4
where the time goes:
time: 751 us
  waiting for transfers between devices  616 us (82%)
  blocking collectives  39.8 us (5%)
  other arithmetic  29.5 us (4%)
  local copies, waits for them, and re-layouts  21.4 us (3%)
  matrix products  19.5 us (3%)
  between operations  13.7 us (2%)
  starting transfers between devices  9.93 us (1%)
    reduce_scatter x1, waiting for transfers between devices, on_device(): lax.psum_scatter(jnp.dot(block, down_weight, preferred_element_type=jnp.f...  216 us
    reduce_scatter x1, waiting for transfers between devices, on_device(): lax.psum_scatter(jnp.dot(block, wo_full, preferred_element_type=jnp.float...  214 us
    all_gather x1, waiting for transfers between devices, on_device(): lax.all_gather(normed, 'hid', axis=0, tiled=True)  78.8 us
    all_gather x1, waiting for transfers between devices, on_device(): group_kv = lax.all_gather(response_kv, 'hid', axis=0, tiled=True)  60.4 us
    all_gather x1, waiting for transfers between devices, combined_all(): gathered = jax.tree.map(lambda a: lax.all_gather(a, axis), part)  34.4 us
    all_gather x2, blocking collectives, combined_all(): gathered = jax.tree.map(lambda a: lax.all_gather(a, axis), part)  26.3 us
    add x7, other arithmetic, join(): first[2] * left[..., None] + second[2] * right[..., None]  15.7 us
  transfers between devices with their start and end apart: 7, of which 6 were waited for; matrix products, arithmetic and copies ran while one was open for 5% of the time, Pallas kernels for 0%

commit v1 on v0

--- a/solution.py
+++ b/solution.py
@@ -1,33 +1,351 @@
+import functools
 import math
 
 import jax
 import jax.numpy as jnp
 from jax import lax
+from jax.experimental import pallas as pl
+from jax.experimental.pallas import tpu as pltpu
 from jax.sharding import PartitionSpec as P
 
 HEADS = 48
 KV_HEADS = 8
 HEAD = 128
 GROUP = 6
-
-
-def combined_all(part, axis, combine):
-    gathered = jax.tree.map(lambda a: lax.all_gather(a, axis), part)
-
-    def take(source):
-        return jax.tree.map(lambda a: lax.dynamic_index_in_dim(a, source, 0, False), gathered)
-
-    return lax.fori_loop(
-        1, lax.axis_size(axis), lambda source, state: combine(state, take(source)), take(0)
-    )
-
-
-def layer_norm(hidden, gain):
-    wide = hidden.astype(jnp.float32)
+D = 6144
+MESH = pl.DeviceIdType.MESH
+BF = jnp.bfloat16
+F32 = jnp.float32
+
+ZI = {0: 0, 1: 1, -1: 2, 2: 3, -2: 4, 3: 5, -3: 6, 4: 7}
+YI = {0: 0, 1: 1, -1: 2, 2: 3}
+ZGROUPS = (pl.ds(0, 1), pl.ds(1, 2), pl.ds(3, 2), pl.ds(5, 2), pl.ds(7, 1))
+
+A_COLS = 2560
+B_COLS = D - A_COLS
+CA, A0, A1 = pl.ds(0, A_COLS), pl.ds(0, A_COLS // 2), pl.ds(A_COLS // 2, A_COLS // 2)
+CB = pl.ds(A_COLS, B_COLS)
+B0, B1 = pl.ds(A_COLS, B_COLS // 2), pl.ds(A_COLS + B_COLS // 2, B_COLS // 2)
+LB, L0, L1 = pl.ds(0, B_COLS), pl.ds(0, B_COLS // 2), pl.ds(B_COLS // 2, B_COLS // 2)
+N_GATHER = 40
+N_REDUCE = 40
+
+
+class Copies:
+    def __init__(self, send_sems, recv_sems):
+        self.sems = send_sems, recv_sems
+        self.made = []
+
+    def send(self, src, dst, device):
+        i = len(self.made)
+        copy = pltpu.make_async_remote_copy(
+            src_ref=src,
+            dst_ref=dst,
+            send_sem=self.sems[0].at[i],
+            recv_sem=self.sems[1].at[i],
+            device_id=device,
+            device_id_type=MESH,
+        )
+        copy.start()
+        self.made.append(copy)
+        return copy
+
+    def finish(self):
+        for copy in self.made:
+            copy.wait_send()
+
+
+def where_am_i():
+    key = lax.axis_index("key")
+    hid = lax.axis_index("hid")
+    return key // 2, key % 2, hid // 4, hid % 4
+
+
+def device(x, core, z, y):
+    return (lax.rem(x, 4) * 2 + core, lax.rem(z, 8) * 4 + lax.rem(y, 4))
+
+
+def greet(devices):
+    barrier = pltpu.get_barrier_semaphore()
+    for one in devices:
+        pl.semaphore_signal(barrier, inc=1, device_id=one, device_id_type=MESH)
+    pl.semaphore_wait(barrier, len(devices))
+
+
+def add_into(dst, *srcs):
+    total = dst[...].astype(F32)
+    for src in srcs:
+        total = total + src[...].astype(F32)
+    dst[...] = total.astype(BF)
+
+
+def ffn_kernel(
+    mid_ref, gain_ref, up_hbm, down_hbm, out_ref,
+    up_w, down_w, rows, part, acc, act,
+    a_zp, a_zm, a_yp, a_ym, b_yp, b_ym, b_zp, b_zm,
+    w_sem, g_send, g_recv, r_send, r_recv,
+):
+    x, core, z, y = where_am_i()
+    zp, zm = device(x, core, z + 1, y), device(x, core, z + 7, y)
+    yp, ym = device(x, core, z, y + 1), device(x, core, z, y + 3)
+    load_up = pltpu.make_async_copy(up_hbm, up_w, w_sem.at[0])
+    load_down = pltpu.make_async_copy(down_hbm, down_w, w_sem.at[1])
+    load_up.start()
+    load_down.start()
+
+    wide = mid_ref[...].astype(F32)
     mean = jnp.mean(wide, axis=-1, keepdims=True)
     centred = wide - mean
     var = jnp.mean(centred * centred, axis=-1, keepdims=True)
-    return (centred * lax.rsqrt(var + 1e-05) * gain).astype(jnp.bfloat16)
+    rows[0, 0] = (centred * lax.rsqrt(var + 1e-05) * gain_ref[...]).astype(BF)
+    greet((zp, zm, yp, ym))
+
+    net = Copies(g_send, g_recv)
+    every = pl.ds(0, 4)
+
+    def ring_next(i, ys, cols, half0, half1):
+        if i == 0:
+            return (
+                net.send(rows.at[0, ys, :, cols], rows.at[ZI[-1], ys, :, cols], zp),
+                net.send(rows.at[0, ys, :, cols], rows.at[ZI[1], ys, :, cols], zm),
+            )
+        if i < 3:
+            return (
+                net.send(rows.at[ZI[-i], ys, :, cols], rows.at[ZI[-i - 1], ys, :, cols], zp),
+                net.send(rows.at[ZI[i], ys, :, cols], rows.at[ZI[i + 1], ys, :, cols], zm),
+            )
+        return (
+            net.send(rows.at[ZI[-3], ys, :, half0], rows.at[ZI[4], ys, :, half0], zp),
+            net.send(rows.at[ZI[3], ys, :, half1], rows.at[ZI[4], ys, :, half1], zm),
+        )
+
+    def arrived(copies):
+        for copy in copies:
+            copy.wait_recv()
+
+    def y_first(zs, cols):
+        return (
+            net.send(rows.at[zs, 0, :, cols], rows.at[zs, YI[-1], :, cols], yp),
+            net.send(rows.at[zs, 0, :, cols], rows.at[zs, YI[1], :, cols], ym),
+        )
+
+    def y_second(zs, half0, half1):
+        return (
+            net.send(rows.at[zs, YI[-1], :, half0], rows.at[zs, YI[2], :, half0], yp),
+            net.send(rows.at[zs, YI[1], :, half1], rows.at[zs, YI[2], :, half1], ym),
+        )
+
+    own = pl.ds(0, 1)
+    ay = y_first(own, CA)
+    bz = ring_next(0, 0, CB, B0, B1)
+    by = [y_first(ZGROUPS[0], CB)]
+    by2 = []
+    arrived(ay)
+    ay = y_second(own, A0, A1)
+    arrived(bz)
+    bz = ring_next(1, 0, CB, B0, B1)
+    by.append(y_first(ZGROUPS[1], CB))
+    arrived(ay)
+    az = ring_next(0, every, CA, A0, A1)
+    arrived(by[0])
+    by2.append(y_second(ZGROUPS[0], B0, B1))
+    arrived(bz)
+    bz = ring_next(2, 0, CB, B0, B1)
+    by.append(y_first(ZGROUPS[2], CB))
+    arrived(by[1])
+    by2.append(y_second(ZGROUPS[1], B0, B1))
+    arrived(az)
+    az = ring_next(1, every, CA, A0, A1)
+    arrived(bz)
+    bz = ring_next(3, 0, CB, B0, B1)
+    by.append(y_first(ZGROUPS[3], CB))
+    arrived(by[2])
+    by2.append(y_second(ZGROUPS[2], B0, B1))
+    arrived(az)
+    az = ring_next(2, every, CA, A0, A1)
+    arrived(bz)
+    by.append(y_first(ZGROUPS[4], CB))
+    arrived(by[3])
+    by2.append(y_second(ZGROUPS[3], B0, B1))
+    arrived(az)
+    az = ring_next(3, every, CA, A0, A1)
+    arrived(by[4])
+    by2.append(y_second(ZGROUPS[4], B0, B1))
+    arrived(az)
+    for pair in by2:
+        arrived(pair)
+
+    load_up.wait()
+    acc[...] = jnp.zeros_like(acc)
+
+    def up_step(i, _):
+        cols = pl.ds(pl.multiple_of(i * 512, 512), 512)
+        block = rows[:, :, :, cols].astype(F32).reshape(256, 512).astype(BF)
+        acc[...] += jnp.dot(block, up_w[cols, :], preferred_element_type=F32)
+        return 0
+
+    lax.fori_loop(0, D // 512, up_step, 0)
+    up = jnp.maximum(acc[...], 0.0)
+    act[...] = (up * up).astype(BF)
+    load_down.wait()
+
+    def down_step(i, _):
+        cols = pl.ds(pl.multiple_of(i * 512, 512), 512)
+        block = jnp.dot(act[...], down_w[:, cols], preferred_element_type=F32)
+        part[:, :, :, cols] = block.reshape(8, 4, 8, 512).astype(BF)
+        return 0
+
+    net.finish()
+    net = Copies(r_send, r_recv)
+
+    def z_send(d, ys, cols, half0, half1, lcols, lh0, lh1, got_p, got_m, lys):
+        if d == 4:
+            return (
+                net.send(part.at[ZI[4], ys, :, half1], got_p.at[3, lys, :, lh1], zp),
+                net.send(part.at[ZI[4], ys, :, half0], got_m.at[3, lys, :, lh0], zm),
+            )
+        return (
+            net.send(part.at[ZI[d], ys, :, cols], got_p.at[d - 1, lys, :, lcols], zp),
+            net.send(part.at[ZI[-d], ys, :, cols], got_m.at[d - 1, lys, :, lcols], zm),
+        )
+
+    def z_add(copies, d, ys, cols, half0, half1, lcols, lh0, lh1, got_p, got_m, lys):
+        arrived(copies)
+        if d == 3:
+            add_into(part.at[ZI[3], ys, :, half1], got_p.at[3, lys, :, lh1])
+            add_into(part.at[ZI[-3], ys, :, half0], got_m.at[3, lys, :, lh0])
+        elif d > 0:
+            add_into(part.at[ZI[d], ys, :, cols], got_p.at[d, lys, :, lcols])
+            add_into(part.at[ZI[-d], ys, :, cols], got_m.at[d, lys, :, lcols])
+        else:
+            add_into(
+                part.at[0, ys, :, cols], got_p.at[0, lys, :, lcols], got_m.at[0, lys, :, lcols]
+            )
+
+    def y_send(step, zs, cols, half0, half1, lcols, lh0, lh1, got_p, got_m):
+        if step == 0:
+            return (
+                net.send(part.at[zs, YI[2], :, half1], got_p.at[1, zs, :, lh1], yp),
+                net.send(part.at[zs, YI[2], :, half0], got_m.at[1, zs, :, lh0], ym),
+            )
+        return (
+            net.send(part.at[zs, YI[1], :, cols], got_p.at[0, zs, :, lcols], yp),
+            net.send(part.at[zs, YI[-1], :, cols], got_m.at[0, zs, :, lcols], ym),
+        )
+
+    def y_add(copies, step, zs, cols, half0, half1, lcols, lh0, lh1, got_p, got_m):
+        arrived(copies)
+        if step == 0:
+            add_into(part.at[zs, YI[1], :, half1], got_p.at[1, zs, :, lh1])
+            add_into(part.at[zs, YI[-1], :, half0], got_m.at[1, zs, :, lh0])
+        else:
+            add_into(part.at[zs, 0, :, cols], got_p.at[0, zs, :, lcols], got_m.at[0, zs, :, lcols])
+
+    za = (every, CA, A0, A1, CA, A0, A1, a_zp, a_zm, every)
+    zb = (0, CB, B0, B1, LB, L0, L1, b_zp, b_zm, 0)
+    yb = (CB, B0, B1, LB, L0, L1, b_yp, b_ym)
+    ya = (CA, A0, A1, CA, A0, A1, a_yp, a_ym)
+
+    lax.fori_loop(A_COLS // 512, D // 512, down_step, 0)
+    order = [ZGROUPS[i] for i in (4, 3, 2, 1, 0)]
+    by = [y_send(0, g, *yb) for g in order]
+    lax.fori_loop(0, A_COLS // 512, down_step, 0)
+    az = z_send(4, *za)
+    y_add(by[0], 0, order[0], *yb)
+    by[0] = y_send(1, order[0], *yb)
+    y_add(by[1], 0, order[1], *yb)
+    by[1] = y_send(1, order[1], *yb)
+    z_add(az, 3, *za)
+    az = z_send(3, *za)
+    y_add(by[2], 0, order[2], *yb)
+    by[2] = y_send(1, order[2], *yb)
+    y_add(by[0], 1, order[0], *yb)
+    bz = z_send(4, *zb)
+    y_add(by[3], 0, order[3], *yb)
+    by[3] = y_send(1, order[3], *yb)
+    z_add(az, 2, *za)
+    az = z_send(2, *za)
+    y_add(by[4], 0, order[4], *yb)
+    by[4] = y_send(1, order[4], *yb)
+    y_add(by[1], 1, order[1], *yb)
+    z_add(bz, 3, *zb)
+    bz = z_send(3, *zb)
+    z_add(az, 1, *za)
+    az = z_send(1, *za)
+    y_add(by[2], 1, order[2], *yb)
+    z_add(bz, 2, *zb)
+    bz = z_send(2, *zb)
+    y_add(by[3], 1, order[3], *yb)
+    z_add(az, 0, *za)
+    ay = y_send(0, own, *ya)
+    z_add(bz, 1, *zb)
+    bz = z_send(1, *zb)
+    y_add(ay, 0, own, *ya)
+    ay = y_send(1, own, *ya)
+    y_add(by[4], 1, order[4], *yb)
+    arrived(bz)
+    out_ref[:, CB] = (
+        mid_ref[:, CB].astype(F32)
+        + part[0, 0, :, CB].astype(F32)
+        + b_zp[0, 0].astype(F32)
+        + b_zm[0, 0].astype(F32)
+    ).astype(BF)
+    arrived(ay)
+    out_ref[:, CA] = (
+        mid_ref[:, CA].astype(F32)
+        + part[0, 0, :, CA].astype(F32)
+        + a_yp[0, 0].astype(F32)
+        + a_ym[0, 0].astype(F32)
+    ).astype(BF)
+    net.finish()
+
+
+def ffn(mid, gain, up_weight, down_weight):
+    vmem = pl.BlockSpec(memory_space=pltpu.VMEM)
+    hbm = pl.BlockSpec(memory_space=pl.ANY)
+    hidden = up_weight.shape[1]
+    return pl.pallas_call(
+        ffn_kernel,
+        name="ffn",
+        out_shape=jax.ShapeDtypeStruct(mid.shape, BF),
+        in_specs=[vmem, vmem, hbm, hbm],
+        out_specs=vmem,
+        scratch_shapes=[
+            pltpu.VMEM((D, hidden), BF),
+            pltpu.VMEM((hidden, D), BF),
+            pltpu.VMEM((8, 4, 8, D), BF),
+            pltpu.VMEM((8, 4, 8, D), BF),
+            pltpu.VMEM((256, hidden), F32),
+            pltpu.VMEM((256, hidden), BF),
+            pltpu.VMEM((4, 4, 8, A_COLS), BF),
+            pltpu.VMEM((4, 4, 8, A_COLS), BF),
+            pltpu.VMEM((2, 1, 8, A_COLS), BF),
+            pltpu.VMEM((2, 1, 8, A_COLS), BF),
+            pltpu.VMEM((2, 8, 8, B_COLS), BF),
+            pltpu.VMEM((2, 8, 8, B_COLS), BF),
+            pltpu.VMEM((4, 1, 8, B_COLS), BF),
+            pltpu.VMEM((4, 1, 8, B_COLS), BF),
+            pltpu.SemaphoreType.DMA((2,)),
+            pltpu.SemaphoreType.DMA((N_GATHER,)),
+            pltpu.SemaphoreType.DMA((N_GATHER,)),
+            pltpu.SemaphoreType.DMA((N_REDUCE,)),
+            pltpu.SemaphoreType.DMA((N_REDUCE,)),
+        ],
+        compiler_params=pltpu.CompilerParams(
+            collective_id=0, has_side_effects=True, vmem_limit_bytes=48 * 1024 * 1024
+        ),
+    )(mid, gain.reshape(1, D), up_weight, down_weight)
+
+
+def combined_all(part, axis, combine):
+    gathered = jax.tree.map(lambda a: lax.all_gather(a, axis), part)
+
+    def take(source):
+        return jax.tree.map(lambda a: lax.dynamic_index_in_dim(a, source, 0, False), gathered)
+
+    return lax.fori_loop(
+        1, lax.axis_size(axis), lambda source, state: combine(state, take(source)), take(0)
+    )
 
 
 def join(first, second):
@@ -113,21 +431,7 @@
         tiled=True,
     ).astype(jnp.float32)
     mid = (residual.astype(jnp.float32) + proj).astype(jnp.bfloat16)
-    normed = layer_norm(mid, norm_gain)
-    up = jnp.dot(
-        lax.all_gather(normed, "hid", axis=0, tiled=True),
-        up_weight,
-        preferred_element_type=jnp.float32,
-    )
-    active = jnp.square(jnp.maximum(up, 0.0)).astype(jnp.bfloat16)
-    block = active
-    down = lax.psum_scatter(
-        jnp.dot(block, down_weight, preferred_element_type=jnp.float32).astype(jnp.bfloat16),
-        "hid",
-        scatter_dimension=0,
-        tiled=True,
-    ).astype(jnp.float32)
-    return (mid.astype(jnp.float32) + down).astype(jnp.bfloat16)
+    return ffn(mid, norm_gain, up_weight, down_weight)
 
 
 def solution(mesh):

time: 751 us -> 512 us (0.68)
  waiting for transfers between devices: 616 us -> 321 us
  Pallas kernels: 0 us -> 66 us
  matrix products: 19.5 us -> 9.69 us
    reduce_scatter x1 -> x0, waiting for transfers between devices: 216 us -> none  [on_device(): lax.psum_scatter(jnp.dot(block, down_weight, preferred_element_type=jnp.f...]
    all_gather x1 -> x0, waiting for transfers between devices: 78.8 us -> none  [on_device(): lax.all_gather(normed, 'hid', axis=0, tiled=True)]
    pallas_call x0 -> x1, Pallas kernels: none -> 66 us  [ffn(): pl.pallas_call(ffn_kernel, name='ffn', out_shape=jax.ShapeDtypeStruct(mid...]
    dot_general x1 -> x0, matrix products: 9.86 us -> none  [on_device(): jnp.dot(block, down_weight, preferred_element_type=jnp.float32)]
  transfers between devices with their start and end apart: 7 -> 5, of which waited for: 6 -> 4; matrix products, arithmetic and copies ran while one was open for 5% -> 7% of each run, Pallas kernels for 0% -> 0%
where the time goes in v1:
time: 512 us; the launch traced here: 511 us
  waiting for transfers between devices  321 us (63%)
  Pallas kernels  66 us (13%)
  blocking collectives  39.8 us (8%)
  other arithmetic  25.5 us (5%)
  local copies, waits for them, and re-layouts  25.4 us (5%)
  between operations  13.4 us (3%)
  starting transfers between devices  9.84 us (2%)
  matrix products  9.69 us (2%)
    reduce_scatter x1, waiting for transfers between devices, on_device(): lax.psum_scatter(jnp.dot(block, wo_full, preferred_element_type=jnp.float...  214 us
    pallas_call x1, Pallas kernels, ffn(): pl.pallas_call(ffn_kernel, name='ffn', out_shape=jax.ShapeDtypeStruct(mid...  66 us
    all_gather x1, waiting for transfers between devices, on_device(): group_kv = lax.all_gather(response_kv, 'hid', axis=0, tiled=True)  60.4 us
    all_gather x1, waiting for transfers between devices, combined_all(): gathered = jax.tree.map(lambda a: lax.all_gather(a, axis), part)  34.4 us
    all_gather x2, blocking collectives, combined_all(): gathered = jax.tree.map(lambda a: lax.all_gather(a, axis), part)  26.3 us
    add x7, other arithmetic, join(): first[2] * left[..., None] + second[2] * right[..., None]  15.7 us
    all_gather x1, blocking collectives, on_device(): lax.all_gather(queries, 'key', axis=0, tiled=True)  13.5 us
    unnamed x19, local copies, waits for them, and re-layouts  13.1 us
  transfers between devices with their start and end apart: 5, of which 4 were waited for; matrix products, arithmetic and copies ran while one was open for 7% of the time, Pallas kernels for 0%

profile of v1, /device:TPU:2, one launch (start us, length us, event | category | flops | bytes accessed | tf_op | source)
XLA Modules:
  0.0 511.1 jit_solution(17037516164457465496)
XLA Ops:
  6.5 0.7 all-gather.4.cloned.1.call-update
  7.3 0.8 dynamic_slice.50
  8.1 1.5 gather_fusion
  9.6 1.7 copy.26
  11.3 13.5 %all_gather.19 = bf16[64,6144]{1,0:T(8,128)(2,1)S(1)} all-gather(bf16[8,6144]{1,0:T(8,128)(2,1)S(1)} %copy-done.5), channel_id=1, replica_groups=mesh['key'=8,'hid'=32] {'key'}, dimensions={0}, use_global_device_ids=true | all-gather | bytes 884736 | tf_op jit(solution)/shard_map/all_gather | solution.py:381
  24.9 2.0 reshape.168
  26.9 1.7 copy.30
  28.6 0.1 and_or_fusion
  28.8 60.4 %all-gather.4.cloned.1.call-done = bf16[256,2048]{1,0:T(8,128)(2,1)} async-done(((bf16[8,2048]{1,0:T(8,128)(2,1)}), bf16[256,2048]{1,0:T(8,128)(2,1)}) %all-gather.4.cloned.1.call-update) | async-done | bytes 1048592 | tf_op jit(solution)/shard_map/all_gather | solution.py:384
  89.1 2.2 fusion.25
  91.4 2.1 copy.46
  93.5 2.1 copy.47
  95.5 1.4 pad_maximum_fusion
  96.9 0.3 pad_maximum_fusion.1
  97.2 0.9 copy-done.3
  98.1 2.6 fusion.5
  100.7 2.8 fusion.3
  103.6 1.7 copy-done.2
  105.2 2.1 copy.32
  107.3 0.7 all-gather.8.cloned.1.call-update
  108.0 6.5 %fusion.4 = f32[64,8,6]{0,2,1:T(8,128)S(1)} fusion(f32[8,1024,64,6]{1,2,3,0:T(8,128)} %copy-done.2, f32[64,8,6]{0,2,1:T(8,128)S(1)} %get-tuple-element.220, pred[64,1024]{1,0:T(8,128)(4,1)S(1)} %and_or_fusion), kind=kLoop, calls=%fused_computation.14 | loop fusion | flops 12579840 | bytes 12673024 | tf_op jit(solution)/shard_map/reduce_sum | solution.py:413
  114.6 13.0 %all_gather.20 = f32[8,64,48]{1,2,0:T(8,128)S(1)} all-gather(f32[1,64,48]{1,2,0:T(8,128)S(1)} %all_gather_reshape.9), channel_id=1, replica_groups=mesh['key'=8,'hid'=32] {'key'}, dimensions={0}, use_global_device_ids=true | all-gather | bytes 110592 | tf_op jit(solution)/shard_map/all_gather | solution.py:341
  127.6 0.1 copy.33
  127.7 13.3 %all_gather.21 = f32[8,64,48]{1,2,0:T(8,128)S(1)} all-gather(f32[1,64,48]{1,2,0:T(8,128)S(1)} %all_gather_reshape.10), channel_id=1, replica_groups=mesh['key'=8,'hid'=32] {'key'}, dimensions={0}, use_global_device_ids=true | all-gather | bytes 110592 | tf_op jit(solution)/shard_map/all_gather | solution.py:341
  140.9 0.1 copy.34
  141.0 34.4 %all-gather.6.cloned.1.call-done = f32[8,64,48,128]{3,2,1,0:T(8,128)} async-done(((f32[1,64,48,128]{3,2,1,0:T(8,128)}), f32[8,64,48,128]{3,2,1,0:T(8,128)}) %all-gather.6.cloned.1.call-update) | async-done | bytes 12582928 | tf_op jit(solution)/shard_map/all_gather | solution.py:341
  175.4 1.5 slice_bitcast_fusion
  176.9 17.5 %while.19 = (s32[]{:T(128)}, f32[64,48]{1,0:T(8,128)S(1)}, f32[64,48]{1,0:T(8,128)S(1)}, f32[64,48,128]{2,1,0:T(8,128)S(1)}, f32[8,64,48]{1,2,0:T(8,128)S(1)}, /...) while((s32[]{:T(128)}, f32[64,48]{1,0:T(8,128)S(1)}, ...), condition=%wide.region_3.4_spmd, body=%wide.region_2.3_spmd.sunk | while | flops 1198085 | bytes 4939927 | solution.py:346
  177.0 0.1 copy.54
  177.2 2.2 fusion.32
  179.7 2.2 fusion.32
  182.2 2.2 fusion.32
  184.7 2.2 fusion.32
  186.9 0.1 copy.54
  187.1 2.2 fusion.32
  189.6 2.3 fusion.32
  192.2 2.2 fusion.32
  194.4 0.1 divide_convert_fusion
  194.6 0.1 convert_element_type.22
  194.7 0.8 copy.37
  195.5 9.7 %all-to-all-start = ((bf16[8,32,192]{2,0,1:T(8,128)(2,1)}), bf16[8,32,192]{2,0,1:T(8,128)(2,1)S(1)}, u32[]{:S(2)}, u32[]{:S(2)}) async-start(bf16[8,32,192]{2,0,1:T(8,128)(2,1)} %copy.37), calls=%async_computation | async-start | bytes 262144 | tf_op jit(solution)/shard_map/all_to_all | solution.py:425
  205.3 10.8 %all-to-all-done = bf16[8,32,192]{2,0,1:T(8,128)(2,1)S(1)} async-done(((bf16[8,32,192]{2,0,1:T(8,128)(2,1)}), bf16[8,32,192]{2,0,1:T(8,128)(2,1)S(1)}, u32[]{:S(2)}, u32[]{:S(2)}) %all-to-all-start) | async-done | bytes 98336 | tf_op jit(solution)/shard_map/all_to_all | solution.py:425
  216.1 4.3 convolution_convert_fusion
  220.4 214.3 %reduce-scatter.2.cloned.1.call-done = bf16[8,6144]{1,0:T(8,128)(2,1)} async-done(((bf16[256,6144]{1,0:T(8,128)(2,1)}), bf16[8,6144]{1,0:T(8,128)(2,1)}) %reduce-scatter.2.cloned.1.call-update) | async-done | bytes 98320 | tf_op jit(solution)/shard_map/reduce_scatter | solution.py:427
  434.7 0.9 add_convert_fusion.mid_ref
  435.6 2.3 copy-done
  438.0 66.0 %ffn.1 = bf16[8,6144]{1,0:T(8,128)(2,1)S(1)} custom-call(bf16[8,6144]{1,0:T(8,128)(2,1)S(1)} %add_convert_fusion.mid_ref, f32[1,6144]{1,0:T(1,128)S(1)} %bitcast.62, bf16[6144,384]{1,0:T(8,128)(2,1)S(1)} %copy-done, bf16[384,6144]{1,0:T(8,128)(2,1)} %down_hbm.1), custom_call_target="tpu_custom_call" | custom-call | tf_op jit(solution)/shard_map/ffn/pallas_call | solution.py:307
  503.9 0.6 copy.69
  (56 shorter events, 1.6 us)
Async XLA Ops:
  6.5 4.8 copy-start.5
  6.5 82.6 %all-gather.4.cloned.1.call-start = ((), (), s32[]{:S(2)}) async-start(), calls=%async_computation.2 | async-start | bytes 1081344 | tf_op jit(solution)/shard_map/all_gather | solution.py:384
  7.3 168.2 %all-gather.6.cloned.1.call-start = ((), (), s32[]{:S(2)}) async-start(), calls=%async_computation.3 | async-start | bytes 14155776 | tf_op jit(solution)/shard_map/all_gather | solution.py:341
  95.5 1.4 copy-start.4
  96.9 1.2 copy-start.3
  100.7 4.5 copy-start.2
  107.3 98.0 %all-gather.8.cloned.1.call-start = ((), (), s32[]{:S(2)}) async-start(), calls=%async_computation.4 | async-start | bytes 2654208 | tf_op jit(solution)/shard_map/all_gather | solution.py:382
  195.5 20.6 %all-to-all-start = ((bf16[8,32,192]{2,0,1:T(8,128)(2,1)}), bf16[8,32,192]{2,0,1:T(8,128)(2,1)S(1)}, u32[]{:S(2)}, u32[]{:S(2)}) async-start(bf16[8,32,192]{2,0,1:T(8,128)(2,1)} %copy.37), calls=%async_computation | async-start | bytes 262144 | tf_op jit(solution)/shard_map/all_to_all | solution.py:425
  205.2 229.5 %copy-start.6 = (bf16[8,6144]{1,0:T(8,128)(2,1)S(1)}, bf16[8,6144]{1,0:T(8,128)(2,1)}, u32[]{:S(2)}) copy-start(bf16[8,6144]{1,0:T(8,128)(2,1)} %param.17) | copy-start | bytes 294916
  205.2 230.4 %copy-start.1 = (f32[6144]{0:T(1024)S(1)}, f32[6144]{0:T(1024)}, u32[]{:S(2)}) copy-start(f32[6144]{0:T(1024)} %param.19) | copy-start | bytes 73732
  205.2 229.5 %reduce-scatter.2.cloned.1.call-start = ((), (), s32[]{:S(2)}) async-start(), calls=%async_computation.5 | async-start | bytes 3244032 | tf_op jit(solution)/shard_map/reduce_scatter | solution.py:427
  435.6 2.3 copy-start
Sparse Core Ops, SparseCore 0:
  9.9 79.1 all-gather.3
  107.4 67.9 all-gather.5
  177.3 27.7 all-gather.7
  220.5 214.1 reduce-scatter.1

commit v2 on v1

--- a/solution.py
+++ b/solution.py
@@ -337,25 +337,252 @@
     )(mid, gain.reshape(1, D), up_weight, down_weight)
 
 
-def combined_all(part, axis, combine):
-    gathered = jax.tree.map(lambda a: lax.all_gather(a, axis), part)
-
-    def take(source):
-        return jax.tree.map(lambda a: lax.dynamic_index_in_dim(a, source, 0, False), gathered)
-
-    return lax.fori_loop(
-        1, lax.axis_size(axis), lambda source, state: combine(state, take(source)), take(0)
+LOG2_SCALE = math.log2(math.e) / math.sqrt(HEAD)
+Q_COLS = GROUP * HEAD
+KEYS_OWN = 768
+KEYS_CHIP = 2 * KEYS_OWN
+RESP = 512
+N_CHIP = 1536
+
+
+def attend_kernel(
+    q_ref, ck_hbm, cv_hbm, rkv_ref, seg_ref, res_ref, wo_hbm, mid_ref,
+    packed, got, qall, rkv, kbuf, vbuf, wo, obuf, stat, robuf, rstat, attn, part, zp_buf, zm_buf,
+    px, local_sem, s_sem, r_sem,
+):
+    x, core, z, y = where_am_i()
+    sib = device(x, 1 - core, z, y)
+    zdev = [device(x, core, z + d, y) for d in range(8)]
+    xdev = [device(x + d, core, z, y) for d in range(4)]
+    ydev = [device(x, core, z, y + d) for d in range(4)]
+    head = pl.ds(pl.multiple_of(z * HEAD, HEAD), HEAD)
+    wo_rows = pl.ds(pl.multiple_of(y * 192, 64), 192)
+    wo_own = pl.ds(pl.multiple_of(core * 768, 128), 768)
+
+    load_k = pltpu.make_async_copy(ck_hbm.at[:, head], kbuf.at[pl.ds(0, KEYS_OWN)], local_sem.at[0])
+    load_v = pltpu.make_async_copy(
+        cv_hbm.at[:, head], vbuf.at[pl.ds(0, KEYS_OWN), pl.ds(0, HEAD)], local_sem.at[1]
     )
-
-
-def join(first, second):
-    top = jnp.maximum(first[0], second[0])
-    left = jnp.exp(first[0] - top)
-    right = jnp.exp(second[0] - top)
-    return (
-        top,
-        first[1] * left + second[1] * right,
-        first[2] * left[..., None] + second[2] * right[..., None],
+    load_wo = pltpu.make_async_copy(wo_hbm, wo.at[wo_rows, wo_own], local_sem.at[2])
+    load_k.start()
+    load_v.start()
+    load_wo.start()
+    for i in range(8):
+        packed[i, :, 0:Q_COLS] = q_ref[:, i * Q_COLS : (i + 1) * Q_COLS]
+        packed[i, :, Q_COLS : Q_COLS + HEAD] = rkv_ref[:, i * HEAD : (i + 1) * HEAD]
+        packed[i, :, Q_COLS + HEAD :] = rkv_ref[:, 1024 + i * HEAD : 1024 + (i + 1) * HEAD]
+    greet([*zdev[1:], *xdev[1:], *ydev[1:], sib])
+    net = Copies(s_sem, r_sem)
+
+    def arrived(copies):
+        for copy in copies:
+            copy.wait_recv()
+
+    moves = [
+        net.send(packed.at[lax.rem(z + d, 8)], got.at[8 - d], zdev[d]) for d in (4, 3, 5, 2, 6, 1, 7)
+    ]
+    caches = [
+        net.send(ck_hbm.at[:, head], kbuf.at[pl.ds(KEYS_OWN, KEYS_OWN)], sib),
+        net.send(cv_hbm.at[:, head], vbuf.at[pl.ds(KEYS_OWN, KEYS_OWN), pl.ds(0, HEAD)], sib),
+    ]
+    got[0] = packed[z]
+    vbuf[:, HEAD:] = jnp.ones((KEYS_CHIP + RESP, HEAD), BF)
+    arrived(moves)
+    rkv[0, 0] = got[:, :, Q_COLS:]
+    kv_moves = [net.send(rkv.at[0, 0], rkv.at[0, 4 - d], ydev[d]) for d in (2, 1, 3)]
+    qall[0] = got[:, :, 0:Q_COLS]
+    q_moves = [net.send(qall.at[0], qall.at[4 - d], xdev[d]) for d in (1, 3, 2)]
+
+    seg = seg_ref[...]
+    bounds = [
+        jnp.sum(jnp.where(seg < s, 1, 0), keepdims=True) for s in (1, 2, 3)
+    ]
+    lanes = lax.broadcasted_iota(jnp.int32, (1, RESP), 1)
+    key_row = (
+        (2 * x + ((core + lanes // 256) & 1)) * 32
+        + ((z + (lanes // 8)) & 7) * 4
+        + ((y + (lanes // 64)) & 3)
+    ) * 8 + (lanes & 7)
+    slots = lax.broadcasted_iota(jnp.int32, (64, 1), 0)
+
+    arrived(kv_moves)
+    kv_sib = net.send(rkv.at[0], rkv.at[1], sib)
+    load_wo.wait()
+    own_wo = wo.at[wo_rows, wo_own]
+    wo_moves = [net.send(own_wo, own_wo, ydev[d]) for d in (1, 3)]
+    load_k.wait()
+    load_v.wait()
+    arrived(caches)
+    arrived([kv_sib])
+    kbuf[pl.ds(KEYS_CHIP, RESP), :] = rkv[:, :, :, :, 0:HEAD].astype(F32).reshape(RESP, HEAD).astype(BF)
+    vbuf[pl.ds(KEYS_CHIP, RESP), 0:HEAD] = (
+        rkv[:, :, :, :, HEAD:].astype(F32).reshape(RESP, HEAD).astype(BF)
+    )
+
+    def attend(i):
+        wide = qall[i].astype(F32)
+        q = jnp.concatenate(
+            [wide[:, :, j * HEAD : (j + 1) * HEAD].reshape(64, HEAD) for j in range(GROUP)], 0
+        ).astype(BF)
+        q_row = ((2 * ((x + i) & 3) + core) * 32 + ((z + slots // 8) & 7) * 4 + y) * 8 + (slots & 7)
+        start = jnp.zeros_like(q_row)
+        for bound in bounds:
+            start = jnp.maximum(start, jnp.where(q_row >= bound, bound, 0))
+        seen = (key_row <= q_row) & (key_row >= start)
+        seen = jnp.concatenate([jnp.where(seen, 0.0, -jnp.inf)] * GROUP, 0)
+        nt = (((1,), (1,)), ((), ()))
+        s1 = lax.dot_general(q, kbuf[0:KEYS_CHIP, :], nt, preferred_element_type=F32)
+        s2 = lax.dot_general(q, kbuf[KEYS_CHIP:, :], nt, preferred_element_type=F32) + seen
+        top = jnp.maximum(
+            jnp.max(s1, axis=-1, keepdims=True), jnp.max(s2, axis=-1, keepdims=True)
+        )
+        p1 = jnp.exp2((s1 - top) * LOG2_SCALE).astype(BF)
+        p2 = jnp.exp2((s2 - top) * LOG2_SCALE).astype(BF)
+        mixed = jnp.dot(p1, vbuf[0:KEYS_CHIP, :], preferred_element_type=F32) + jnp.dot(
+            p2, vbuf[KEYS_CHIP:, :], preferred_element_type=F32
+        )
+        lane = lax.broadcasted_iota(jnp.int32, (64, HEAD), 1)
+        tops = jnp.zeros((64, HEAD), F32)
+        totals = jnp.ones((64, HEAD), F32)
+        for j in range(GROUP):
+            rows = slice(j * 64, (j + 1) * 64)
+            obuf[i, :, :, j * HEAD : (j + 1) * HEAD] = mixed[rows, 0:HEAD].reshape(8, 8, HEAD).astype(BF)
+            tops = jnp.where(lane == j, top[rows], tops)
+            totals = jnp.where(lane == j, mixed[rows, HEAD:], totals)
+        stat[i, 0] = tops
+        stat[i, 1] = totals
+
+    o_moves = []
+
+    def give(d):
+        attend(d)
+        o_moves.append(net.send(obuf.at[d], robuf.at[4 - d], xdev[d]))
+        o_moves.append(net.send(stat.at[d], rstat.at[4 - d], xdev[d]))
+
+    arrived([q_moves[2]])
+    give(2)
+    arrived([q_moves[0]])
+    give(3)
+    arrived(wo_moves)
+    back, ahead = lax.rem(y + 3, 4), lax.rem(y + 1, 4)
+    low = wo.at[pl.ds(pl.multiple_of(back * 192, 64), 96), wo_own]
+    high = wo.at[pl.ds(pl.multiple_of(ahead * 192 + 96, 32), 96), wo_own]
+    wo_moves = [net.send(low, low, ydev[1]), net.send(high, high, ydev[3])]
+    arrived([q_moves[1]])
+    give(1)
+    attend(0)
+    arrived(wo_moves)
+    wo_cols = wo.at[:, wo_own]
+    wo_sib = net.send(wo_cols, wo_cols, sib)
+    arrived(o_moves)
+
+    tops = [stat[0, 0]] + [rstat[i, 0] for i in range(1, 4)]
+    totals = [stat[0, 1]] + [rstat[i, 1] for i in range(1, 4)]
+    top = functools.reduce(jnp.maximum, tops)
+    scales = [jnp.exp2((t - top) * LOG2_SCALE) for t in tops]
+    total = functools.reduce(jnp.add, [a * b for a, b in zip(scales, totals)])
+    scales = [a / total for a in scales]
+    for j in range(GROUP):
+        cols = slice(j * HEAD, (j + 1) * HEAD)
+        mixed = obuf[0, :, :, cols].astype(F32).reshape(64, HEAD) * scales[0][:, j : j + 1]
+        for i in range(1, 4):
+            mixed = mixed + robuf[i, :, :, cols].astype(F32).reshape(64, HEAD) * scales[i][:, j : j + 1]
+        attn[0, :, :, cols] = mixed.reshape(8, 8, HEAD).astype(BF)
+    a_moves = [net.send(attn.at[0], attn.at[4 - d], xdev[d]) for d in (2, 1, 3)]
+    arrived([wo_sib])
+    arrived(a_moves)
+
+    lhs = attn[...].astype(F32).reshape(256, Q_COLS).astype(BF)
+    ring = [[], []]
+
+    def z_cols(p):
+        base = p * 768
+        return pl.ds(base, 768), pl.ds(base, 384), pl.ds(base + 384, 384)
+
+    def z_send(p, d):
+        cols, half0, half1 = z_cols(p)
+        if d == 4:
+            ring[p] = [
+                net.send(part.at[4, :, :, half1], zp_buf.at[3, :, :, half1], zdev[1]),
+                net.send(part.at[4, :, :, half0], zm_buf.at[3, :, :, half0], zdev[7]),
+            ]
+        else:
+            ring[p] = [
+                net.send(part.at[d, :, :, cols], zp_buf.at[d - 1, :, :, cols], zdev[1]),
+                net.send(part.at[8 - d, :, :, cols], zm_buf.at[d - 1, :, :, cols], zdev[7]),
+            ]
+
+    def z_add(p, d):
+        cols, half0, half1 = z_cols(p)
+        arrived(ring[p])
+        if d == 3:
+            add_into(part.at[3, :, :, half1], zp_buf.at[3, :, :, half1])
+            add_into(part.at[5, :, :, half0], zm_buf.at[3, :, :, half0])
+        elif d > 0:
+            add_into(part.at[d, :, :, cols], zp_buf.at[d, :, :, cols])
+            add_into(part.at[8 - d, :, :, cols], zm_buf.at[d, :, :, cols])
+        else:
+            add_into(part.at[0, :, :, cols], zp_buf.at[0, :, :, cols], zm_buf.at[0, :, :, cols])
+
+    for p in range(2):
+        cols = slice(p * 768, (p + 1) * 768)
+        block = jnp.dot(lhs, wo[:, cols], preferred_element_type=F32).reshape(4, 8, 8, 768)
+        for i in range(4):
+            part[:, i, :, cols] = block[i].astype(BF)
+        z_send(p, 4)
+    for d in (3, 2, 1):
+        for p in range(2):
+            z_add(p, d)
+            z_send(p, d)
+    p_moves = []
+    for p in range(2):
+        z_add(p, 0)
+        cols = z_cols(p)[0]
+        for d in (2, 1, 3):
+            p_moves.append(net.send(part.at[0, d, :, cols], px.at[4 - d, :, cols], xdev[d]))
+    px[0] = part[0, 0]
+    arrived(p_moves)
+    for i in range(4):
+        cols = pl.ds(pl.multiple_of(((x + i) & 3) * N_CHIP, HEAD), N_CHIP)
+        mid_ref[:, cols] = (res_ref[:, cols].astype(F32) + px[i].astype(F32)).astype(BF)
+    net.finish()
+
+
+def attend(queries, cache_keys, cache_values, response_kv, segments, residual, out_weight):
+    vmem = pl.BlockSpec(memory_space=pltpu.VMEM)
+    hbm = pl.BlockSpec(memory_space=pl.ANY)
+    return pl.pallas_call(
+        attend_kernel,
+        name="attend",
+        out_shape=jax.ShapeDtypeStruct(residual.shape, BF),
+        in_specs=[vmem, hbm, hbm, vmem, vmem, vmem, hbm],
+        out_specs=vmem,
+        scratch_shapes=[
+            pltpu.VMEM((8, 8, 1024), BF),
+            pltpu.VMEM((8, 8, 1024), BF),
+            pltpu.VMEM((4, 8, 8, Q_COLS), BF),
+            pltpu.VMEM((2, 4, 8, 8, 2 * HEAD), BF),
+            pltpu.VMEM((KEYS_CHIP + RESP, HEAD), BF),
+            pltpu.VMEM((KEYS_CHIP + RESP, 2 * HEAD), BF),
+            pltpu.VMEM((Q_COLS, N_CHIP), BF),
+            pltpu.VMEM((4, 8, 8, Q_COLS), BF),
+            pltpu.VMEM((4, 2, 64, HEAD), F32),
+            pltpu.VMEM((4, 8, 8, Q_COLS), BF),
+            pltpu.VMEM((4, 2, 64, HEAD), F32),
+            pltpu.VMEM((4, 8, 8, Q_COLS), BF),
+            pltpu.VMEM((8, 4, 8, N_CHIP), BF),
+            pltpu.VMEM((4, 4, 8, N_CHIP), BF),
+            pltpu.VMEM((4, 4, 8, N_CHIP), BF),
+            pltpu.VMEM((4, 8, N_CHIP), BF),
+            pltpu.SemaphoreType.DMA((3,)),
+            pltpu.SemaphoreType.DMA((64,)),
+            pltpu.SemaphoreType.DMA((64,)),
+        ],
+        compiler_params=pltpu.CompilerParams(
+            collective_id=1, has_side_effects=True, vmem_limit_bytes=48 * 1024 * 1024
+        ),
+    )(
+        queries, cache_keys, cache_values, response_kv, segments.reshape(16, 128), residual, out_weight
     )
 
 
@@ -371,66 +598,9 @@
     up_weight,
     down_weight,
 ):
-    n_hid = lax.axis_size("hid")
-    key_idx = lax.axis_index("key")
-    hid_idx = lax.axis_index("hid")
-    tok = queries.shape[0]
-    width = cache_keys.shape[1]
-    ctx_dev = cache_keys.shape[0]
-    q_all, wo_full = (
-        lax.all_gather(queries, "key", axis=0, tiled=True),
-        lax.all_gather(out_weight, "key", axis=1, tiled=True),
+    mid = attend(
+        queries, cache_keys, cache_values, response_kv, segments, residual, out_weight
     )
-    group_kv = lax.all_gather(response_kv, "hid", axis=0, tiled=True)
-    group_rows = group_kv.shape[0]
-    keys = jnp.concatenate([cache_keys, group_kv[:, :width]], 0).reshape(-1, KV_HEADS, HEAD)
-    values = (
-        jnp.concatenate([cache_values, group_kv[:, width:]], 0)
-        .astype(jnp.float32)
-        .reshape(-1, KV_HEADS, HEAD)
-    )
-    key_rows = jnp.concatenate(
-        [
-            jnp.full((ctx_dev,), -1, jnp.int32),
-            key_idx * group_rows + jnp.arange(group_rows, dtype=jnp.int32),
-        ]
-    )
-    own_seg = lax.dynamic_slice_in_dim(segments, key_idx * group_rows, group_rows)
-    key_seg = jnp.concatenate([jnp.full((ctx_dev,), -1, jnp.int32), own_seg])
-    count = q_all.shape[0]
-    slot = jnp.arange(count, dtype=jnp.int32)
-    q_rows = (slot // tok * n_hid + hid_idx) * tok + slot % tok
-    q_seg = jnp.take(segments, q_rows)
-    scale = 1.0 / math.sqrt(HEAD)
-    grouped = q_all.reshape(count, KV_HEADS, GROUP, HEAD)
-    score = jnp.einsum("bgjd,ngd->bgjn", grouped, keys, preferred_element_type=jnp.float32) * scale
-    seen = (key_rows[None, :] < 0) | (key_seg[None, :] == q_seg[:, None]) & (
-        key_rows[None, :] <= q_rows[:, None]
-    )
-    score = jnp.where(seen[:, None, None, :], score, -jnp.inf)
-    top = jnp.max(score, axis=-1)
-    weight = jnp.exp(score - top[..., None])
-    summed = jnp.sum(weight, axis=-1)
-    mixed = jnp.einsum("bgjn,ngd->bgjd", weight, values)
-    top = top.reshape(count, HEADS)
-    summed = summed.reshape(count, HEADS)
-    mixed = mixed.reshape(count, HEADS, HEAD)
-    top_all, sum_all, mix_all = combined_all((top, summed, mixed), "key", join)
-    own = (
-        lax.dynamic_slice_in_dim(top_all, key_idx * tok, tok, 0),
-        lax.dynamic_slice_in_dim(sum_all, key_idx * tok, tok, 0),
-        lax.dynamic_slice_in_dim(mix_all, key_idx * tok, tok, 0),
-    )
-    attn = (own[2] / own[1][..., None]).reshape(tok, HEADS * HEAD).astype(jnp.bfloat16)
-    attn_cols = lax.all_to_all(attn, "hid", split_axis=1, concat_axis=0, tiled=True)
-    block = attn_cols
-    proj = lax.psum_scatter(
-        jnp.dot(block, wo_full, preferred_element_type=jnp.float32).astype(jnp.bfloat16),
-        "hid",
-        scatter_dimension=0,
-        tiled=True,
-    ).astype(jnp.float32)
-    mid = (residual.astype(jnp.float32) + proj).astype(jnp.bfloat16)
     return ffn(mid, norm_gain, up_weight, down_weight)
 
 

time: 512 us -> 138 us (0.27)
  waiting for transfers between devices: 321 us -> 0 us
  Pallas kernels: 66 us -> 125 us
  blocking collectives: 39.8 us -> 0 us
  other arithmetic: 25.5 us -> 0 us
  local copies, waits for them, and re-layouts: 25.4 us -> 10.7 us
  between operations: 13.4 us -> 0.03 us
  starting transfers between devices: 9.84 us -> 0 us
  matrix products: 9.69 us -> 0 us
    reduce_scatter x1 -> x0, waiting for transfers between devices: 214 us -> none  [on_device(): lax.psum_scatter(jnp.dot(block, wo_full, preferred_element_type=jnp.float...]
    all_gather x3 -> x0, waiting for transfers between devices: 94.8 us -> none  [the longest x1 60.4 us: on_device(): group_kv = lax.all_gather(response_kv, 'hid', axis=0, tiled=True)]
    pallas_call x0 -> x1, Pallas kernels: none -> 58 us  [attend(): pl.pallas_call(attend_kernel, name='attend', out_shape=jax.ShapeDtypeStru...]
    all_gather x3 -> x0, blocking collectives: 39.8 us -> none  [the longest x2 26.3 us: combined_all(): gathered = jax.tree.map(lambda a: lax.all_gather(a, axis), part)]
    add x15 -> x0, other arithmetic: 16 us -> none  [the longest x7 15.7 us: join(): first[2] * left[..., None] + second[2] * right[..., None]]
    all_to_all x1 -> x0, waiting for transfers between devices: 10.8 us -> none  [on_device(): lax.all_to_all(attn, 'hid', split_axis=1, concat_axis=0, tiled=True)]
    all_to_all x1 -> x0, starting transfers between devices: 9.72 us -> none  [on_device(): lax.all_to_all(attn, 'hid', split_axis=1, concat_axis=0, tiled=True)]
    dot_general x3 -> x0, matrix products: 9.69 us -> none  [the longest x1 4.3 us: on_device(): jnp.dot(block, wo_full, preferred_element_type=jnp.float32)]
  transfers between devices with their start and end apart: 5 -> 0, of which waited for: 4 -> 0; matrix products, arithmetic and copies ran while one was open for 7% -> 0% of each run, Pallas kernels for 0% -> 0%
where the time goes in v2:
time: 138 us; the launch traced here: 136 us
  Pallas kernels  125 us (91%)
  local copies, waits for them, and re-layouts  10.7 us (8%)
    pallas_call x1, Pallas kernels, ffn(): pl.pallas_call(ffn_kernel, name='ffn', out_shape=jax.ShapeDtypeStruct(mid...  67.5 us
    pallas_call x1, Pallas kernels, attend(): pl.pallas_call(attend_kernel, name='attend', out_shape=jax.ShapeDtypeStru...  58 us
    unnamed x19, local copies, waits for them, and re-layouts  10.7 us

profile of v2, /device:TPU:2, one launch (start us, length us, event | category | flops | bytes accessed | tf_op | source)
XLA Modules:
  0.0 136.2 jit_solution(4251847351245438371)
XLA Ops:
  0.0 0.0 copy-start.1
  0.0 1.4 %copy-done.1 = bf16[768,1024]{1,0:T(8,128)(2,1)S(1)} copy-done((bf16[768,1024]{1,0:T(8,128)(2,1)S(1)}, bf16[768,1024]{1,0:T(8,128)(2,1)}, u32[]{:S(2)}) %copy-start.1) | copy-done | bytes 1572888
  1.4 0.0 copy-start.2
  1.4 1.4 %copy-done.2 = bf16[768,1024]{1,0:T(8,128)(2,1)S(1)} copy-done((bf16[768,1024]{1,0:T(8,128)(2,1)S(1)}, bf16[768,1024]{1,0:T(8,128)(2,1)}, u32[]{:S(2)}) %copy-start.2) | copy-done | bytes 1572888
  2.8 0.0 copy-start.3
  2.8 1.0 copy-done.3
  3.8 0.0 copy-start.4
  3.8 0.9 copy-done.4
  4.7 0.0 copy-start.5
  4.7 0.9 copy-done.5
  5.6 0.0 copy-start.6
  5.6 0.8 copy-done.6
  6.3 0.0 copy-start.8
  6.3 0.7 copy-done.8
  7.0 58.0 %attend.1.mid_ref = bf16[8,6144]{1,0:T(8,128)(2,1)S(1)} custom-call(bf16[8,6144]{1,0:T(8,128)(2,1)S(1)} %copy-done.4, bf16[768,1024]{1,0:T(8,128)(2,1)S(1)} %copy-done.1, bf16[768,1024]{1,0:T(8,128)(2,1)S(1)} %copy-done.2, bf16[8,2048]{1,0:T(8,128)(2,1)S(1)} %copy-done.6, s32[16,128]{1,0:T(8,128)S(1)} %bitcast.3, bf16[8,6144]{1,0:T(8,128)(2,1)S(1)} %copy-done.5, ...), custom_call_target="tpu_custom_call" | custom-call | tf_op jit(solution)/shard_map/attend/pallas_call | solution.py:554
  65.0 0.0 copy-start
  65.0 2.3 %copy-done = bf16[6144,384]{1,0:T(8,128)(2,1)S(1)} copy-done((bf16[6144,384]{1,0:T(8,128)(2,1)S(1)}, bf16[6144,384]{1,0:T(8,128)(2,1)}, u32[]{:S(2)}) %copy-start) | copy-done | bytes 4718616
  67.4 0.0 copy-start.7
  67.4 0.7 copy-done.7
  68.1 67.5 %ffn.1 = bf16[8,6144]{1,0:T(8,128)(2,1)S(1)} custom-call(bf16[8,6144]{1,0:T(8,128)(2,1)S(1)} %attend.1.mid_ref, f32[1,6144]{1,0:T(1,128)S(1)} %bitcast.2, bf16[6144,384]{1,0:T(8,128)(2,1)S(1)} %copy-done, bf16[384,6144]{1,0:T(8,128)(2,1)} %down_hbm.1), custom_call_target="tpu_custom_call" | custom-call | tf_op jit(solution)/shard_map/ffn/pallas_call | solution.py:307
  135.6 0.6 copy.12
Async XLA Ops:
  0.0 1.4 %copy-start.1 = (bf16[768,1024]{1,0:T(8,128)(2,1)S(1)}, bf16[768,1024]{1,0:T(8,128)(2,1)}, u32[]{:S(2)}) copy-start(bf16[768,1024]{1,0:T(8,128)(2,1)} %ck_hbm.1) | copy-start | bytes 4718596
  1.4 1.4 %copy-start.2 = (bf16[768,1024]{1,0:T(8,128)(2,1)S(1)}, bf16[768,1024]{1,0:T(8,128)(2,1)}, u32[]{:S(2)}) copy-start(bf16[768,1024]{1,0:T(8,128)(2,1)} %cv_hbm.1) | copy-start | bytes 4718596
  2.8 1.0 copy-start.3
  3.8 0.9 copy-start.4
  4.7 0.9 copy-start.5
  5.6 0.8 copy-start.6
  6.3 0.7 copy-start.8
  65.0 2.3 %copy-start = (bf16[6144,384]{1,0:T(8,128)(2,1)S(1)}, bf16[6144,384]{1,0:T(8,128)(2,1)}, u32[]{:S(2)}) copy-start(bf16[6144,384]{1,0:T(8,128)(2,1)} %up_hbm.1) | copy-start | bytes 14155780
  67.4 0.7 copy-start.7

commit v3 on v2

--- a/solution.py
+++ b/solution.py
@@ -79,26 +79,21 @@
     dst[...] = total.astype(BF)
 
 
-def ffn_kernel(
-    mid_ref, gain_ref, up_hbm, down_hbm, out_ref,
+def ffn_phase(
+    where, mid_ref, gain_ref, load_up, load_down, out_ref,
     up_w, down_w, rows, part, acc, act,
     a_zp, a_zm, a_yp, a_ym, b_yp, b_ym, b_zp, b_zm,
-    w_sem, g_send, g_recv, r_send, r_recv,
+    g_send, g_recv, r_send, r_recv,
 ):
-    x, core, z, y = where_am_i()
+    x, core, z, y = where
     zp, zm = device(x, core, z + 1, y), device(x, core, z + 7, y)
     yp, ym = device(x, core, z, y + 1), device(x, core, z, y + 3)
-    load_up = pltpu.make_async_copy(up_hbm, up_w, w_sem.at[0])
-    load_down = pltpu.make_async_copy(down_hbm, down_w, w_sem.at[1])
-    load_up.start()
-    load_down.start()
 
     wide = mid_ref[...].astype(F32)
     mean = jnp.mean(wide, axis=-1, keepdims=True)
     centred = wide - mean
     var = jnp.mean(centred * centred, axis=-1, keepdims=True)
     rows[0, 0] = (centred * lax.rsqrt(var + 1e-05) * gain_ref[...]).astype(BF)
-    greet((zp, zm, yp, ym))
 
     net = Copies(g_send, g_recv)
     every = pl.ds(0, 4)
@@ -300,43 +295,6 @@
     net.finish()
 
 
-def ffn(mid, gain, up_weight, down_weight):
-    vmem = pl.BlockSpec(memory_space=pltpu.VMEM)
-    hbm = pl.BlockSpec(memory_space=pl.ANY)
-    hidden = up_weight.shape[1]
-    return pl.pallas_call(
-        ffn_kernel,
-        name="ffn",
-        out_shape=jax.ShapeDtypeStruct(mid.shape, BF),
-        in_specs=[vmem, vmem, hbm, hbm],
-        out_specs=vmem,
-        scratch_shapes=[
-            pltpu.VMEM((D, hidden), BF),
-            pltpu.VMEM((hidden, D), BF),
-            pltpu.VMEM((8, 4, 8, D), BF),
-            pltpu.VMEM((8, 4, 8, D), BF),
-            pltpu.VMEM((256, hidden), F32),
-            pltpu.VMEM((256, hidden), BF),
-            pltpu.VMEM((4, 4, 8, A_COLS), BF),
-            pltpu.VMEM((4, 4, 8, A_COLS), BF),
-            pltpu.VMEM((2, 1, 8, A_COLS), BF),
-            pltpu.VMEM((2, 1, 8, A_COLS), BF),
-            pltpu.VMEM((2, 8, 8, B_COLS), BF),
-            pltpu.VMEM((2, 8, 8, B_COLS), BF),
-            pltpu.VMEM((4, 1, 8, B_COLS), BF),
-            pltpu.VMEM((4, 1, 8, B_COLS), BF),
-            pltpu.SemaphoreType.DMA((2,)),
-            pltpu.SemaphoreType.DMA((N_GATHER,)),
-            pltpu.SemaphoreType.DMA((N_GATHER,)),
-            pltpu.SemaphoreType.DMA((N_REDUCE,)),
-            pltpu.SemaphoreType.DMA((N_REDUCE,)),
-        ],
-        compiler_params=pltpu.CompilerParams(
-            collective_id=0, has_side_effects=True, vmem_limit_bytes=48 * 1024 * 1024
-        ),
-    )(mid, gain.reshape(1, D), up_weight, down_weight)
-
-
 LOG2_SCALE = math.log2(math.e) / math.sqrt(HEAD)
 Q_COLS = GROUP * HEAD
 KEYS_OWN = 768
@@ -345,10 +303,11 @@
 N_CHIP = 1536
 
 
-def attend_kernel(
-    q_ref, ck_hbm, cv_hbm, rkv_ref, seg_ref, res_ref, wo_hbm, mid_ref,
+def layer_kernel(
+    q_hbm, ck_hbm, cv_hbm, rkv_hbm, seg_hbm, res_hbm, wo_hbm, gain_hbm, up_hbm, down_hbm, out_ref,
+    q_ref, rkv_ref, seg_ref, res_ref, gain_ref, mid_ref, up_w, down_w,
     packed, got, qall, rkv, kbuf, vbuf, wo, obuf, stat, robuf, rstat, attn, part, zp_buf, zm_buf,
-    px, local_sem, s_sem, r_sem,
+    px, local_sem, s_sem, r_sem, *ffn_refs,
 ):
     x, core, z, y = where_am_i()
     sib = device(x, 1 - core, z, y)
@@ -359,6 +318,23 @@
     wo_rows = pl.ds(pl.multiple_of(y * 192, 64), 192)
     wo_own = pl.ds(pl.multiple_of(core * 768, 128), 768)
 
+    loads = [
+        pltpu.make_async_copy(src, dst, local_sem.at[3 + i])
+        for i, (src, dst) in enumerate(
+            (
+                (q_hbm, q_ref),
+                (rkv_hbm, rkv_ref),
+                (seg_hbm, seg_ref),
+                (res_hbm, res_ref),
+                (gain_hbm, gain_ref),
+                (up_hbm, up_w),
+                (down_hbm, down_w),
+            )
+        )
+    ]
+    load_q, load_rkv, load_seg, load_res, load_gain, load_up, load_down = loads
+    load_q.start()
+    load_rkv.start()
     load_k = pltpu.make_async_copy(ck_hbm.at[:, head], kbuf.at[pl.ds(0, KEYS_OWN)], local_sem.at[0])
     load_v = pltpu.make_async_copy(
         cv_hbm.at[:, head], vbuf.at[pl.ds(0, KEYS_OWN), pl.ds(0, HEAD)], local_sem.at[1]
@@ -367,6 +343,10 @@
     load_k.start()
     load_v.start()
     load_wo.start()
+    for load in (load_seg, load_res, load_gain):
+        load.start()
+    load_q.wait()
+    load_rkv.wait()
     for i in range(8):
         packed[i, :, 0:Q_COLS] = q_ref[:, i * Q_COLS : (i + 1) * Q_COLS]
         packed[i, :, Q_COLS : Q_COLS + HEAD] = rkv_ref[:, i * HEAD : (i + 1) * HEAD]
@@ -393,6 +373,7 @@
     qall[0] = got[:, :, 0:Q_COLS]
     q_moves = [net.send(qall.at[0], qall.at[4 - d], xdev[d]) for d in (1, 3, 2)]
 
+    load_seg.wait()
     seg = seg_ref[...]
     bounds = [
         jnp.sum(jnp.where(seg < s, 1, 0), keepdims=True) for s in (1, 2, 3)
@@ -405,6 +386,8 @@
     ) * 8 + (lanes & 7)
     slots = lax.broadcasted_iota(jnp.int32, (64, 1), 0)
 
+    load_up.start()
+    load_down.start()
     arrived(kv_moves)
     kv_sib = net.send(rkv.at[0], rkv.at[1], sib)
     load_wo.wait()
@@ -541,23 +524,47 @@
         for d in (2, 1, 3):
             p_moves.append(net.send(part.at[0, d, :, cols], px.at[4 - d, :, cols], xdev[d]))
     px[0] = part[0, 0]
+    load_res.wait()
+    load_gain.wait()
     arrived(p_moves)
     for i in range(4):
         cols = pl.ds(pl.multiple_of(((x + i) & 3) * N_CHIP, HEAD), N_CHIP)
         mid_ref[:, cols] = (res_ref[:, cols].astype(F32) + px[i].astype(F32)).astype(BF)
     net.finish()
-
-
-def attend(queries, cache_keys, cache_values, response_kv, segments, residual, out_weight):
-    vmem = pl.BlockSpec(memory_space=pltpu.VMEM)
+    ffn_phase(
+        (x, core, z, y), mid_ref, gain_ref, load_up, load_down, out_ref, up_w, down_w, *ffn_refs
+    )
+
+
+def on_device(
+    queries,
+    cache_keys,
+    cache_values,
+    response_kv,
+    segments,
+    residual,
+    out_weight,
+    norm_gain,
+    up_weight,
+    down_weight,
+):
     hbm = pl.BlockSpec(memory_space=pl.ANY)
+    hidden = up_weight.shape[1]
     return pl.pallas_call(
-        attend_kernel,
-        name="attend",
+        layer_kernel,
+        name="layer",
         out_shape=jax.ShapeDtypeStruct(residual.shape, BF),
-        in_specs=[vmem, hbm, hbm, vmem, vmem, vmem, hbm],
-        out_specs=vmem,
+        in_specs=[hbm] * 10,
+        out_specs=pl.BlockSpec(memory_space=pltpu.VMEM),
         scratch_shapes=[
+            pltpu.VMEM(queries.shape, BF),
+            pltpu.VMEM(response_kv.shape, BF),
+            pltpu.VMEM((16, 128), jnp.int32),
+            pltpu.VMEM(residual.shape, BF),
+            pltpu.VMEM((1, D), F32),
+            pltpu.VMEM(residual.shape, BF),
+            pltpu.VMEM((D, hidden), BF),
+            pltpu.VMEM((hidden, D), BF),
             pltpu.VMEM((8, 8, 1024), BF),
             pltpu.VMEM((8, 8, 1024), BF),
             pltpu.VMEM((4, 8, 8, Q_COLS), BF),
@@ -574,34 +581,33 @@
             pltpu.VMEM((4, 4, 8, N_CHIP), BF),
             pltpu.VMEM((4, 4, 8, N_CHIP), BF),
             pltpu.VMEM((4, 8, N_CHIP), BF),
-            pltpu.SemaphoreType.DMA((3,)),
+            pltpu.SemaphoreType.DMA((10,)),
             pltpu.SemaphoreType.DMA((64,)),
             pltpu.SemaphoreType.DMA((64,)),
+            pltpu.VMEM((8, 4, 8, D), BF),
+            pltpu.VMEM((8, 4, 8, D), BF),
+            pltpu.VMEM((256, hidden), F32),
+            pltpu.VMEM((256, hidden), BF),
+            pltpu.VMEM((4, 4, 8, A_COLS), BF),
+            pltpu.VMEM((4, 4, 8, A_COLS), BF),
+            pltpu.VMEM((2, 1, 8, A_COLS), BF),
+            pltpu.VMEM((2, 1, 8, A_COLS), BF),
+            pltpu.VMEM((2, 8, 8, B_COLS), BF),
+            pltpu.VMEM((2, 8, 8, B_COLS), BF),
+            pltpu.VMEM((4, 1, 8, B_COLS), BF),
+            pltpu.VMEM((4, 1, 8, B_COLS), BF),
+            pltpu.SemaphoreType.DMA((N_GATHER,)),
+            pltpu.SemaphoreType.DMA((N_GATHER,)),
+            pltpu.SemaphoreType.DMA((N_REDUCE,)),
+            pltpu.SemaphoreType.DMA((N_REDUCE,)),
         ],
         compiler_params=pltpu.CompilerParams(
-            collective_id=1, has_side_effects=True, vmem_limit_bytes=48 * 1024 * 1024
+            collective_id=0, has_side_effects=True, vmem_limit_bytes=60 * 1024 * 1024
         ),
     )(
-        queries, cache_keys, cache_values, response_kv, segments.reshape(16, 128), residual, out_weight
+        queries, cache_keys, cache_values, response_kv, segments.reshape(16, 128), residual,
+        out_weight, norm_gain.reshape(1, D), up_weight, down_weight,
     )
-
-
-def on_device(
-    queries,
-    cache_keys,
-    cache_values,
-    response_kv,
-    segments,
-    residual,
-    out_weight,
-    norm_gain,
-    up_weight,
-    down_weight,
-):
-    mid = attend(
-        queries, cache_keys, cache_values, response_kv, segments, residual, out_weight
-    )
-    return ffn(mid, norm_gain, up_weight, down_weight)
 
 
 def solution(mesh):

time: 138 us -> 128 us (0.928)
  local copies, waits for them, and re-layouts: 10.7 us -> 1.54 us
    unnamed x19 -> x1, local copies, waits for them, and re-layouts: 10.7 us -> 1.54 us
    pallas_call x2 -> x1, Pallas kernels: 125 us -> 124 us  [on_device(): pl.pallas_call(layer_kernel, name='layer', out_shape=jax.ShapeDtypeStruct...]
where the time goes in v3:
time: 128 us; the launch traced here: 126 us
  Pallas kernels  124 us (97%)
  local copies, waits for them, and re-layouts  1.54 us (1%)
    pallas_call x1, Pallas kernels, on_device(): pl.pallas_call(layer_kernel, name='layer', out_shape=jax.ShapeDtypeStruct...  124 us

profile of v3, /device:TPU:2, one launch (start us, length us, event | category | flops | bytes accessed | tf_op | source)
XLA Modules:
  0.0 125.6 jit_solution(5149615488382425903)
XLA Ops:
  0.0 124.0 %layer.1 = bf16[8,6144]{1,0:T(8,128)(2,1)} custom-call(bf16[8,6144]{1,0:T(8,128)(2,1)} %q_hbm.1, bf16[768,1024]{1,0:T(8,128)(2,1)} %ck_hbm.1, bf16[768,1024]{1,0:T(8,128)(2,1)} %cv_hbm.1, bf16[8,2048]{1,0:T(8,128)(2,1)} %rkv_hbm.1, s32[16,128]{1,0:T(8,128)} %bitcast.3, bf16[8,6144]{1,0:T(8,128)(2,1)} %res_hbm.1, bf16[192,768]{1,0:T(8,128)(2,1)} %wo_hbm.1, ...), custom_call_target="tpu_custom_call" | custom-call | tf_op jit(solution)/shard_map/layer/pallas_call | solution.py:553
  124.0 1.5 %copy.12 = bf16[8,6144]{1,0:T(8,128)(2,1)} copy(bf16[8,6144]{1,0:T(8,128)(2,1)} %layer.1) | data formatting | bytes 196608

commit v4 on v3

--- a/solution.py
+++ b/solution.py
@@ -27,8 +27,8 @@
 CB = pl.ds(A_COLS, B_COLS)
 B0, B1 = pl.ds(A_COLS, B_COLS // 2), pl.ds(A_COLS + B_COLS // 2, B_COLS // 2)
 LB, L0, L1 = pl.ds(0, B_COLS), pl.ds(0, B_COLS // 2), pl.ds(B_COLS // 2, B_COLS // 2)
-N_GATHER = 40
-N_REDUCE = 40
+N_GATHER = 56
+N_REDUCE = 56
 
 
 class Copies:
@@ -69,7 +69,7 @@
     barrier = pltpu.get_barrier_semaphore()
     for one in devices:
         pl.semaphore_signal(barrier, inc=1, device_id=one, device_id_type=MESH)
-    pl.semaphore_wait(barrier, len(devices))
+    return lambda: pl.semaphore_wait(barrier, len(devices))
 
 
 def add_into(dst, *srcs):
@@ -77,6 +77,17 @@
     for src in srcs:
         total = total + src[...].astype(F32)
     dst[...] = total.astype(BF)
+
+
+GATHER_ORDER = (
+    "ay1 bz1 by10 az10 ay2 az11 by11 bz2 by20 az20 az12 az21 by21 bz3 az30 by12 az22 az31 "
+    "bz4 az40 by13 az32 by22 az41 by14 az42 up by23 by24"
+)
+REDUCE_ORDER = (
+    "az42 az41 by04 az40 by03 by02 by01 az32 by00 by14 az31 az30 az22 by13 bz4 by12 az21 az20 "
+    "az12 by11 bz3 by10 az11 ay0 az10 bz2 ay1 bz1"
+)
+PIECES = (pl.ds(0, 1), pl.ds(1, 2), pl.ds(3, 1))
 
 
 def ffn_phase(
@@ -96,27 +107,18 @@
     rows[0, 0] = (centred * lax.rsqrt(var + 1e-05) * gain_ref[...]).astype(BF)
 
     net = Copies(g_send, g_recv)
-    every = pl.ds(0, 4)
-
-    def ring_next(i, ys, cols, half0, half1):
-        if i == 0:
+    flying = {}
+
+    def z_hop(hop, ys, cols, half0, half1):
+        if hop == 4:
             return (
-                net.send(rows.at[0, ys, :, cols], rows.at[ZI[-1], ys, :, cols], zp),
-                net.send(rows.at[0, ys, :, cols], rows.at[ZI[1], ys, :, cols], zm),
-            )
-        if i < 3:
-            return (
-                net.send(rows.at[ZI[-i], ys, :, cols], rows.at[ZI[-i - 1], ys, :, cols], zp),
-                net.send(rows.at[ZI[i], ys, :, cols], rows.at[ZI[i + 1], ys, :, cols], zm),
+                net.send(rows.at[ZI[-3], ys, :, half0], rows.at[ZI[4], ys, :, half0], zp),
+                net.send(rows.at[ZI[3], ys, :, half1], rows.at[ZI[4], ys, :, half1], zm),
             )
         return (
-            net.send(rows.at[ZI[-3], ys, :, half0], rows.at[ZI[4], ys, :, half0], zp),
-            net.send(rows.at[ZI[3], ys, :, half1], rows.at[ZI[4], ys, :, half1], zm),
-        )
-
-    def arrived(copies):
-        for copy in copies:
-            copy.wait_recv()
+            net.send(rows.at[ZI[1 - hop], ys, :, cols], rows.at[ZI[-hop], ys, :, cols], zp),
+            net.send(rows.at[ZI[hop - 1], ys, :, cols], rows.at[ZI[hop], ys, :, cols], zm),
+        )
 
     def y_first(zs, cols):
         return (
@@ -130,68 +132,64 @@
             net.send(rows.at[zs, YI[1], :, half1], rows.at[zs, YI[2], :, half1], ym),
         )
 
+    def az_hop(hop, piece):
+        flying["az%d%d" % (hop, piece)] = z_hop(hop, PIECES[piece], CA, A0, A1)
+
+    def bz_hop(hop):
+        flying["bz%d" % hop] = z_hop(hop, 0, CB, B0, B1)
+
+    def up_cols(first, size, fresh):
+        cols = pl.ds(first, size)
+        block = rows[:, :, :, cols].astype(F32).reshape(256, size).astype(BF)
+        product = jnp.dot(block, up_w[cols, :], preferred_element_type=F32)
+        if fresh:
+            acc[...] = product
+        else:
+            acc[...] += product
+
     own = pl.ds(0, 1)
-    ay = y_first(own, CA)
-    bz = ring_next(0, 0, CB, B0, B1)
-    by = [y_first(ZGROUPS[0], CB)]
-    by2 = []
-    arrived(ay)
-    ay = y_second(own, A0, A1)
-    arrived(bz)
-    bz = ring_next(1, 0, CB, B0, B1)
-    by.append(y_first(ZGROUPS[1], CB))
-    arrived(ay)
-    az = ring_next(0, every, CA, A0, A1)
-    arrived(by[0])
-    by2.append(y_second(ZGROUPS[0], B0, B1))
-    arrived(bz)
-    bz = ring_next(2, 0, CB, B0, B1)
-    by.append(y_first(ZGROUPS[2], CB))
-    arrived(by[1])
-    by2.append(y_second(ZGROUPS[1], B0, B1))
-    arrived(az)
-    az = ring_next(1, every, CA, A0, A1)
-    arrived(bz)
-    bz = ring_next(3, 0, CB, B0, B1)
-    by.append(y_first(ZGROUPS[3], CB))
-    arrived(by[2])
-    by2.append(y_second(ZGROUPS[2], B0, B1))
-    arrived(az)
-    az = ring_next(2, every, CA, A0, A1)
-    arrived(bz)
-    by.append(y_first(ZGROUPS[4], CB))
-    arrived(by[3])
-    by2.append(y_second(ZGROUPS[3], B0, B1))
-    arrived(az)
-    az = ring_next(3, every, CA, A0, A1)
-    arrived(by[4])
-    by2.append(y_second(ZGROUPS[4], B0, B1))
-    arrived(az)
-    for pair in by2:
-        arrived(pair)
-
-    load_up.wait()
-    acc[...] = jnp.zeros_like(acc)
-
-    def up_step(i, _):
-        cols = pl.ds(pl.multiple_of(i * 512, 512), 512)
-        block = rows[:, :, :, cols].astype(F32).reshape(256, 512).astype(BF)
-        acc[...] += jnp.dot(block, up_w[cols, :], preferred_element_type=F32)
-        return 0
-
-    lax.fori_loop(0, D // 512, up_step, 0)
+    flying["ay1"] = y_first(own, CA)
+    bz_hop(1)
+    flying["by10"] = y_first(ZGROUPS[0], CB)
+    az_hop(1, 0)
+    for name in GATHER_ORDER.split():
+        if name == "up":
+            load_up.wait()
+            for i in range(2):
+                up_cols(i * (A_COLS // 2), A_COLS // 2, i == 0)
+            continue
+        for copy in flying[name]:
+            copy.wait_recv()
+        kind, step = name[:2], int(name[2])
+        if kind == "ay" and step == 1:
+            flying["ay2"] = y_second(own, A0, A1)
+            az_hop(1, 1)
+        elif kind == "ay":
+            az_hop(1, 2)
+        elif kind == "az" and step < 4:
+            az_hop(step + 1, int(name[3]))
+        elif kind == "bz":
+            if step < 4:
+                bz_hop(step + 1)
+            flying["by1%d" % step] = y_first(ZGROUPS[step], CB)
+        elif kind == "by" and step == 1:
+            flying["by2" + name[3]] = y_second(ZGROUPS[int(name[3])], B0, B1)
+
+    for i in range(2):
+        up_cols(A_COLS + i * (B_COLS // 2), B_COLS // 2, False)
     up = jnp.maximum(acc[...], 0.0)
     act[...] = (up * up).astype(BF)
     load_down.wait()
 
-    def down_step(i, _):
-        cols = pl.ds(pl.multiple_of(i * 512, 512), 512)
+    def down_cols(first, size):
+        cols = pl.ds(first, size)
         block = jnp.dot(act[...], down_w[:, cols], preferred_element_type=F32)
-        part[:, :, :, cols] = block.reshape(8, 4, 8, 512).astype(BF)
-        return 0
+        part[:, :, :, cols] = block.reshape(8, 4, 8, size).astype(BF)
 
     net.finish()
     net = Copies(r_send, r_recv)
+    flying = {}
+    done = set()
 
     def z_send(d, ys, cols, half0, half1, lcols, lh0, lh1, got_p, got_m, lys):
         if d == 4:
@@ -204,8 +202,7 @@
             net.send(part.at[ZI[-d], ys, :, cols], got_m.at[d - 1, lys, :, lcols], zm),
         )
 
-    def z_add(copies, d, ys, cols, half0, half1, lcols, lh0, lh1, got_p, got_m, lys):
-        arrived(copies)
+    def z_add(d, ys, cols, half0, half1, lcols, lh0, lh1, got_p, got_m, lys):
         if d == 3:
             add_into(part.at[ZI[3], ys, :, half1], got_p.at[3, lys, :, lh1])
             add_into(part.at[ZI[-3], ys, :, half0], got_m.at[3, lys, :, lh0])
@@ -228,70 +225,66 @@
             net.send(part.at[zs, YI[-1], :, cols], got_m.at[0, zs, :, lcols], ym),
         )
 
-    def y_add(copies, step, zs, cols, half0, half1, lcols, lh0, lh1, got_p, got_m):
-        arrived(copies)
+    def y_add(step, zs, cols, half0, half1, lcols, lh0, lh1, got_p, got_m):
         if step == 0:
             add_into(part.at[zs, YI[1], :, half1], got_p.at[1, zs, :, lh1])
             add_into(part.at[zs, YI[-1], :, half0], got_m.at[1, zs, :, lh0])
         else:
             add_into(part.at[zs, 0, :, cols], got_p.at[0, zs, :, lcols], got_m.at[0, zs, :, lcols])
 
-    za = (every, CA, A0, A1, CA, A0, A1, a_zp, a_zm, every)
+    za = [(p, CA, A0, A1, CA, A0, A1, a_zp, a_zm, p) for p in PIECES]
     zb = (0, CB, B0, B1, LB, L0, L1, b_zp, b_zm, 0)
     yb = (CB, B0, B1, LB, L0, L1, b_yp, b_ym)
     ya = (CA, A0, A1, CA, A0, A1, a_yp, a_ym)
 
-    lax.fori_loop(A_COLS // 512, D // 512, down_step, 0)
-    order = [ZGROUPS[i] for i in (4, 3, 2, 1, 0)]
-    by = [y_send(0, g, *yb) for g in order]
-    lax.fori_loop(0, A_COLS // 512, down_step, 0)
-    az = z_send(4, *za)
-    y_add(by[0], 0, order[0], *yb)
-    by[0] = y_send(1, order[0], *yb)
-    y_add(by[1], 0, order[1], *yb)
-    by[1] = y_send(1, order[1], *yb)
-    z_add(az, 3, *za)
-    az = z_send(3, *za)
-    y_add(by[2], 0, order[2], *yb)
-    by[2] = y_send(1, order[2], *yb)
-    y_add(by[0], 1, order[0], *yb)
-    bz = z_send(4, *zb)
-    y_add(by[3], 0, order[3], *yb)
-    by[3] = y_send(1, order[3], *yb)
-    z_add(az, 2, *za)
-    az = z_send(2, *za)
-    y_add(by[4], 0, order[4], *yb)
-    by[4] = y_send(1, order[4], *yb)
-    y_add(by[1], 1, order[1], *yb)
-    z_add(bz, 3, *zb)
-    bz = z_send(3, *zb)
-    z_add(az, 1, *za)
-    az = z_send(1, *za)
-    y_add(by[2], 1, order[2], *yb)
-    z_add(bz, 2, *zb)
-    bz = z_send(2, *zb)
-    y_add(by[3], 1, order[3], *yb)
-    z_add(az, 0, *za)
-    ay = y_send(0, own, *ya)
-    z_add(bz, 1, *zb)
-    bz = z_send(1, *zb)
-    y_add(ay, 0, own, *ya)
-    ay = y_send(1, own, *ya)
-    y_add(by[4], 1, order[4], *yb)
-    arrived(bz)
-    out_ref[:, CB] = (
-        mid_ref[:, CB].astype(F32)
-        + part[0, 0, :, CB].astype(F32)
-        + b_zp[0, 0].astype(F32)
-        + b_zm[0, 0].astype(F32)
-    ).astype(BF)
-    arrived(ay)
-    out_ref[:, CA] = (
-        mid_ref[:, CA].astype(F32)
-        + part[0, 0, :, CA].astype(F32)
-        + a_yp[0, 0].astype(F32)
-        + a_ym[0, 0].astype(F32)
-    ).astype(BF)
+    for i in range(2):
+        down_cols(i * (A_COLS // 2), A_COLS // 2)
+    for p in (2, 1, 0):
+        flying["az4%d" % p] = z_send(4, *za[p])
+    for i in range(2):
+        down_cols(A_COLS + i * (B_COLS // 2), B_COLS // 2)
+    for g in (4, 3, 2, 1, 0):
+        flying["by0%d" % g] = y_send(0, ZGROUPS[g], *yb)
+    for name in REDUCE_ORDER.split():
+        for copy in flying[name]:
+            copy.wait_recv()
+        done.add(name)
+        kind, step = name[:2], int(name[2])
+        if kind == "az":
+            p = int(name[3])
+            z_add(step - 1, *za[p])
+            if step > 1:
+                flying["az%d%d" % (step - 1, p)] = z_send(step - 1, *za[p])
+            elif p == 2:
+                flying["ay0"] = y_send(0, own, *ya)
+        elif kind == "by" and step == 0:
+            y_add(0, ZGROUPS[int(name[3])], *yb)
+            flying["by1" + name[3]] = y_send(1, ZGROUPS[int(name[3])], *yb)
+        elif kind == "by":
+            y_add(1, ZGROUPS[int(name[3])], *yb)
+        elif kind == "bz" and step > 1:
+            z_add(step - 1, *zb)
+        elif kind == "ay" and step == 0:
+            y_add(0, own, *ya)
+        for d in (4, 3, 2, 1):
+            if "bz%d" % d not in flying and "by1%d" % d in done and (d == 4 or "bz%d" % (d + 1) in done):
+                flying["bz%d" % d] = z_send(d, *zb)
+        if "ay1" not in flying and "ay0" in done and "az11" in done:
+            flying["ay1"] = y_send(1, own, *ya)
+        if name == "ay1":
+            out_ref[:, CA] = (
+                mid_ref[:, CA].astype(F32)
+                + part[0, 0, :, CA].astype(F32)
+                + a_yp[0, 0].astype(F32)
+                + a_ym[0, 0].astype(F32)
+            ).astype(BF)
+        if name == "bz1":
+            out_ref[:, CB] = (
+                mid_ref[:, CB].astype(F32)
+                + part[0, 0, :, CB].astype(F32)
+                + b_zp[0, 0].astype(F32)
+                + b_zm[0, 0].astype(F32)
+            ).astype(BF)
     net.finish()
 
 
@@ -306,7 +299,7 @@
 def layer_kernel(
     q_hbm, ck_hbm, cv_hbm, rkv_hbm, seg_hbm, res_hbm, wo_hbm, gain_hbm, up_hbm, down_hbm, out_ref,
     q_ref, rkv_ref, seg_ref, res_ref, gain_ref, mid_ref, up_w, down_w,
-    packed, got, qall, rkv, kbuf, vbuf, wo, obuf, stat, robuf, rstat, attn, part, zp_buf, zm_buf,
+    packed, got, qcat, osum, qall, rkv, kbuf, vbuf, wo, obuf, stat, robuf, rstat, attn, part, zp_buf, zm_buf,
     px, local_sem, s_sem, r_sem, *ffn_refs,
 ):
     x, core, z, y = where_am_i()
@@ -314,6 +307,8 @@
     zdev = [device(x, core, z + d, y) for d in range(8)]
     xdev = [device(x + d, core, z, y) for d in range(4)]
     ydev = [device(x, core, z, y + d) for d in range(4)]
+    ysib = [device(x, 1 - core, z, y + d) for d in range(4)]
+    all_here = greet([*zdev[1:], *xdev[1:], *ydev[1:], *ysib])
     head = pl.ds(pl.multiple_of(z * HEAD, HEAD), HEAD)
     wo_rows = pl.ds(pl.multiple_of(y * 192, 64), 192)
     wo_own = pl.ds(pl.multiple_of(core * 768, 128), 768)
@@ -351,7 +346,7 @@
         packed[i, :, 0:Q_COLS] = q_ref[:, i * Q_COLS : (i + 1) * Q_COLS]
         packed[i, :, Q_COLS : Q_COLS + HEAD] = rkv_ref[:, i * HEAD : (i + 1) * HEAD]
         packed[i, :, Q_COLS + HEAD :] = rkv_ref[:, 1024 + i * HEAD : 1024 + (i + 1) * HEAD]
-    greet([*zdev[1:], *xdev[1:], *ydev[1:], sib])
+    all_here()
     net = Copies(s_sem, r_sem)
 
     def arrived(copies):
@@ -370,6 +365,7 @@
     arrived(moves)
     rkv[0, 0] = got[:, :, Q_COLS:]
     kv_moves = [net.send(rkv.at[0, 0], rkv.at[0, 4 - d], ydev[d]) for d in (2, 1, 3)]
+    kv_moves += [net.send(rkv.at[0, 0], rkv.at[1, (4 - d) % 4], ysib[d]) for d in (2, 1, 3, 0)]
     qall[0] = got[:, :, 0:Q_COLS]
     q_moves = [net.send(qall.at[0], qall.at[4 - d], xdev[d]) for d in (1, 3, 2)]
 
@@ -388,43 +384,37 @@
 
     load_up.start()
     load_down.start()
-    arrived(kv_moves)
-    kv_sib = net.send(rkv.at[0], rkv.at[1], sib)
-    load_wo.wait()
-    own_wo = wo.at[wo_rows, wo_own]
-    wo_moves = [net.send(own_wo, own_wo, ydev[d]) for d in (1, 3)]
-    load_k.wait()
-    load_v.wait()
-    arrived(caches)
-    arrived([kv_sib])
-    kbuf[pl.ds(KEYS_CHIP, RESP), :] = rkv[:, :, :, :, 0:HEAD].astype(F32).reshape(RESP, HEAD).astype(BF)
-    vbuf[pl.ds(KEYS_CHIP, RESP), 0:HEAD] = (
-        rkv[:, :, :, :, HEAD:].astype(F32).reshape(RESP, HEAD).astype(BF)
-    )
-
-    def attend(i):
+    nt = (((1,), (1,)), ((), ()))
+    lane = lax.broadcasted_iota(jnp.int32, (64, HEAD), 1)
+    wide_lane = lax.broadcasted_iota(jnp.int32, (GROUP * 64, HEAD), 1)
+
+    def attend_cache(i):
         wide = qall[i].astype(F32)
         q = jnp.concatenate(
             [wide[:, :, j * HEAD : (j + 1) * HEAD].reshape(64, HEAD) for j in range(GROUP)], 0
         ).astype(BF)
+        qcat[i] = q
+        score = lax.dot_general(q, kbuf[0:KEYS_CHIP, :], nt, preferred_element_type=F32)
+        top = jnp.max(score, axis=-1, keepdims=True)
+        weight = jnp.exp2((score - top) * LOG2_SCALE).astype(BF)
+        mixed = jnp.dot(weight, vbuf[0:KEYS_CHIP, :], preferred_element_type=F32)
+        osum[i, :, 0:HEAD] = mixed[:, 0:HEAD]
+        osum[i, :, HEAD:] = jnp.where(wide_lane < 64, mixed[:, HEAD:], top)
+
+    def attend_response(i):
         q_row = ((2 * ((x + i) & 3) + core) * 32 + ((z + slots // 8) & 7) * 4 + y) * 8 + (slots & 7)
         start = jnp.zeros_like(q_row)
         for bound in bounds:
             start = jnp.maximum(start, jnp.where(q_row >= bound, bound, 0))
         seen = (key_row <= q_row) & (key_row >= start)
         seen = jnp.concatenate([jnp.where(seen, 0.0, -jnp.inf)] * GROUP, 0)
-        nt = (((1,), (1,)), ((), ()))
-        s1 = lax.dot_general(q, kbuf[0:KEYS_CHIP, :], nt, preferred_element_type=F32)
-        s2 = lax.dot_general(q, kbuf[KEYS_CHIP:, :], nt, preferred_element_type=F32) + seen
-        top = jnp.maximum(
-            jnp.max(s1, axis=-1, keepdims=True), jnp.max(s2, axis=-1, keepdims=True)
-        )
-        p1 = jnp.exp2((s1 - top) * LOG2_SCALE).astype(BF)
-        p2 = jnp.exp2((s2 - top) * LOG2_SCALE).astype(BF)
-        mixed = jnp.dot(p1, vbuf[0:KEYS_CHIP, :], preferred_element_type=F32) + jnp.dot(
-            p2, vbuf[KEYS_CHIP:, :], preferred_element_type=F32
-        )
-        lane = lax.broadcasted_iota(jnp.int32, (64, HEAD), 1)
+        score = lax.dot_general(qcat[i], kbuf[KEYS_CHIP:, :], nt, preferred_element_type=F32) + seen
+        first_top = osum[i, :, 2 * HEAD - 1 : 2 * HEAD]
+        top = jnp.maximum(first_top, jnp.max(score, axis=-1, keepdims=True))
+        weight = jnp.exp2((score - top) * LOG2_SCALE).astype(BF)
+        mixed = osum[i] * jnp.exp2((first_top - top) * LOG2_SCALE) + jnp.dot(
+            weight, vbuf[KEYS_CHIP:, :], preferred_element_type=F32
+        )
         tops = jnp.zeros((64, HEAD), F32)
         totals = jnp.ones((64, HEAD), F32)
         for j in range(GROUP):
@@ -438,22 +428,37 @@
     o_moves = []
 
     def give(d):
-        attend(d)
+        attend_response(d)
         o_moves.append(net.send(obuf.at[d], robuf.at[4 - d], xdev[d]))
         o_moves.append(net.send(stat.at[d], rstat.at[4 - d], xdev[d]))
 
+    load_k.wait()
+    load_v.wait()
+    arrived(caches)
+    attend_cache(0)
+    load_wo.wait()
+    own_wo = wo.at[wo_rows, wo_own]
+    wo_moves = [net.send(own_wo, own_wo, ydev[d]) for d in (1, 3)]
+    arrived([q_moves[0]])
+    attend_cache(3)
+    arrived([q_moves[1]])
+    attend_cache(1)
     arrived([q_moves[2]])
+    attend_cache(2)
+    arrived(kv_moves)
+    kbuf[pl.ds(KEYS_CHIP, RESP), :] = rkv[:, :, :, :, 0:HEAD].astype(F32).reshape(RESP, HEAD).astype(BF)
+    vbuf[pl.ds(KEYS_CHIP, RESP), 0:HEAD] = (
+        rkv[:, :, :, :, HEAD:].astype(F32).reshape(RESP, HEAD).astype(BF)
+    )
     give(2)
-    arrived([q_moves[0]])
     give(3)
+    give(1)
     arrived(wo_moves)
     back, ahead = lax.rem(y + 3, 4), lax.rem(y + 1, 4)
     low = wo.at[pl.ds(pl.multiple_of(back * 192, 64), 96), wo_own]
     high = wo.at[pl.ds(pl.multiple_of(ahead * 192 + 96, 32), 96), wo_own]
     wo_moves = [net.send(low, low, ydev[1]), net.send(high, high, ydev[3])]
-    arrived([q_moves[1]])
-    give(1)
-    attend(0)
+    attend_response(0)
     arrived(wo_moves)
     wo_cols = wo.at[:, wo_own]
     wo_sib = net.send(wo_cols, wo_cols, sib)
@@ -567,6 +572,8 @@
             pltpu.VMEM((hidden, D), BF),
             pltpu.VMEM((8, 8, 1024), BF),
             pltpu.VMEM((8, 8, 1024), BF),
+            pltpu.VMEM((4, GROUP * 64, HEAD), BF),
+            pltpu.VMEM((4, GROUP * 64, 2 * HEAD), F32),
             pltpu.VMEM((4, 8, 8, Q_COLS), BF),
             pltpu.VMEM((2, 4, 8, 8, 2 * HEAD), BF),
             pltpu.VMEM((KEYS_CHIP + RESP, HEAD), BF),

time: 128 us -> 113 us (0.88); the launches traced: 126 us -> 113 us
  Pallas kernels: 124 us -> 111 us
    pallas_call x1, Pallas kernels: 124 us -> 111 us  [on_device(): pl.pallas_call(layer_kernel, name='layer', out_shape=jax.ShapeDtypeStruct...]
where the time goes in v4:
time: 113 us
  Pallas kernels  111 us (98%)
  local copies, waits for them, and re-layouts  1.54 us (1%)
    pallas_call x1, Pallas kernels, on_device(): pl.pallas_call(layer_kernel, name='layer', out_shape=jax.ShapeDtypeStruct...  111 us

profile of v4, /device:TPU:2, one launch (start us, length us, event | category | flops | bytes accessed | tf_op | source)
XLA Modules:
  0.0 112.7 jit_solution(10049863181496206286)
XLA Ops:
  0.0 111.2 %layer.1 = bf16[8,6144]{1,0:T(8,128)(2,1)} custom-call(bf16[8,6144]{1,0:T(8,128)(2,1)} %q_hbm.1, bf16[768,1024]{1,0:T(8,128)(2,1)} %ck_hbm.1, bf16[768,1024]{1,0:T(8,128)(2,1)} %cv_hbm.1, bf16[8,2048]{1,0:T(8,128)(2,1)} %rkv_hbm.1, s32[16,128]{1,0:T(8,128)} %bitcast.3, bf16[8,6144]{1,0:T(8,128)(2,1)} %res_hbm.1, bf16[192,768]{1,0:T(8,128)(2,1)} %wo_hbm.1, ...), custom_call_target="tpu_custom_call" | custom-call | tf_op jit(solution)/shard_map/layer/pallas_call | solution.py:558
  111.2 1.5 %copy.12 = bf16[8,6144]{1,0:T(8,128)(2,1)} copy(bf16[8,6144]{1,0:T(8,128)(2,1)} %layer.1) | data formatting | bytes 196608

commit v5 on v4

--- a/solution.py
+++ b/solution.py
@@ -80,12 +80,14 @@
 
 
 GATHER_ORDER = (
-    "ay1 bz1 by10 az10 ay2 az11 by11 bz2 by20 az20 az12 az21 by21 bz3 az30 by12 az22 az31 "
-    "bz4 az40 by13 az32 by22 az41 by14 az42 up by23 by24"
+    "ay1", "bz1", "by10", "az10", "ay2", "az11", "by11", "bz2", "by20", "az20", "az12", "az21",
+    "by21", "bz3", "az30", "by12", "az22", "az31", "bz4", "az40", "by13", "az32", "by22", "az41",
+    "by14", "az42", "up", "upb", "by23", "by24",
 )
 REDUCE_ORDER = (
-    "az42 az41 by04 az40 by03 by02 by01 az32 by00 by14 az31 az30 az22 by13 bz4 by12 az21 az20 "
-    "az12 by11 bz3 by10 az11 ay0 az10 bz2 ay1 bz1"
+    "az42", "az41", "by04", "az40", "by03", "by02", "by01", "az32", "by00", "by14", "az31", "az30",
+    "az22", "by13", "bz4", "by12", "az21", "az20", "az12", "by11", "bz3", "by10", "az11", "ay0",
+    "az10", "bz2", "ay1", "bz1",
 )
 PIECES = (pl.ds(0, 1), pl.ds(1, 2), pl.ds(3, 1))
 
@@ -138,25 +140,30 @@
     def bz_hop(hop):
         flying["bz%d" % hop] = z_hop(hop, 0, CB, B0, B1)
 
-    def up_cols(first, size, fresh):
+    def up_cols(first, size, fresh, low=0, high=8):
         cols = pl.ds(first, size)
-        block = rows[:, :, :, cols].astype(F32).reshape(256, size).astype(BF)
+        count = (high - low) * 32
+        block = rows[low:high, :, :, cols].astype(F32).reshape(count, size).astype(BF)
         product = jnp.dot(block, up_w[cols, :], preferred_element_type=F32)
         if fresh:
-            acc[...] = product
+            acc[low * 32 : high * 32] = product
         else:
-            acc[...] += product
+            acc[low * 32 : high * 32] += product
 
     own = pl.ds(0, 1)
     flying["ay1"] = y_first(own, CA)
     bz_hop(1)
     flying["by10"] = y_first(ZGROUPS[0], CB)
     az_hop(1, 0)
-    for name in GATHER_ORDER.split():
+    for name in GATHER_ORDER:
         if name == "up":
             load_up.wait()
             for i in range(2):
                 up_cols(i * (A_COLS // 2), A_COLS // 2, i == 0)
+            continue
+        if name == "upb":
+            for i in range(2):
+                up_cols(A_COLS + i * (B_COLS // 2), B_COLS // 2, False, 0, 5)
             continue
         for copy in flying[name]:
             copy.wait_recv()
@@ -176,7 +183,7 @@
             flying["by2" + name[3]] = y_second(ZGROUPS[int(name[3])], B0, B1)
 
     for i in range(2):
-        up_cols(A_COLS + i * (B_COLS // 2), B_COLS // 2, False)
+        up_cols(A_COLS + i * (B_COLS // 2), B_COLS // 2, False, 5, 8)
     up = jnp.maximum(acc[...], 0.0)
     act[...] = (up * up).astype(BF)
     load_down.wait()
@@ -245,7 +252,7 @@
         down_cols(A_COLS + i * (B_COLS // 2), B_COLS // 2)
     for g in (4, 3, 2, 1, 0):
         flying["by0%d" % g] = y_send(0, ZGROUPS[g], *yb)
-    for name in REDUCE_ORDER.split():
+    for name in REDUCE_ORDER:
         for copy in flying[name]:
             copy.wait_recv()
         done.add(name)
@@ -415,15 +422,16 @@
         mixed = osum[i] * jnp.exp2((first_top - top) * LOG2_SCALE) + jnp.dot(
             weight, vbuf[KEYS_CHIP:, :], preferred_element_type=F32
         )
-        tops = jnp.zeros((64, HEAD), F32)
-        totals = jnp.ones((64, HEAD), F32)
+        both = jnp.ones((64, HEAD), F32)
         for j in range(GROUP):
             rows = slice(j * 64, (j + 1) * 64)
             obuf[i, :, :, j * HEAD : (j + 1) * HEAD] = mixed[rows, 0:HEAD].reshape(8, 8, HEAD).astype(BF)
-            tops = jnp.where(lane == j, top[rows], tops)
-            totals = jnp.where(lane == j, mixed[rows, HEAD:], totals)
-        stat[i, 0] = tops
-        stat[i, 1] = totals
+            both = jnp.where((lane & 31) == j, top[rows], both)
+            both = jnp.where((lane & 31) == 8 + j, mixed[rows, HEAD : HEAD + 1], both)
+        for g in range(4):
+            quarter = both[g * 16 : (g + 1) * 16]
+            packed_stat = quarter if g == 0 else jnp.where(lane[0:16] >= 32 * g, quarter, packed_stat)
+        stat[i] = packed_stat
 
     o_moves = []
 
@@ -439,10 +447,6 @@
     load_wo.wait()
     own_wo = wo.at[wo_rows, wo_own]
     wo_moves = [net.send(own_wo, own_wo, ydev[d]) for d in (1, 3)]
-    arrived([q_moves[0]])
-    attend_cache(3)
-    arrived([q_moves[1]])
-    attend_cache(1)
     arrived([q_moves[2]])
     attend_cache(2)
     arrived(kv_moves)
@@ -451,7 +455,11 @@
         rkv[:, :, :, :, HEAD:].astype(F32).reshape(RESP, HEAD).astype(BF)
     )
     give(2)
+    arrived([q_moves[0]])
+    attend_cache(3)
     give(3)
+    arrived([q_moves[1]])
+    attend_cache(1)
     give(1)
     arrived(wo_moves)
     back, ahead = lax.rem(y + 3, 4), lax.rem(y + 1, 4)
@@ -464,8 +472,13 @@
     wo_sib = net.send(wo_cols, wo_cols, sib)
     arrived(o_moves)
 
-    tops = [stat[0, 0]] + [rstat[i, 0] for i in range(1, 4)]
-    totals = [stat[0, 1]] + [rstat[i, 1] for i in range(1, 4)]
+    def unpacked(tile, shift):
+        parts = [(tile, (HEAD - 32 * g - shift) % HEAD) for g in range(4)]
+        return jnp.concatenate([pltpu.roll(t, by, 1) if by else t for t, by in parts], 0)
+
+    tiles = [stat[0]] + [rstat[i] for i in range(1, 4)]
+    tops = [unpacked(t, 0) for t in tiles]
+    totals = [unpacked(t, 8) for t in tiles]
     top = functools.reduce(jnp.maximum, tops)
     scales = [jnp.exp2((t - top) * LOG2_SCALE) for t in tops]
     total = functools.reduce(jnp.add, [a * b for a, b in zip(scales, totals)])
@@ -478,56 +491,62 @@
         attn[0, :, :, cols] = mixed.reshape(8, 8, HEAD).astype(BF)
     a_moves = [net.send(attn.at[0], attn.at[4 - d], xdev[d]) for d in (2, 1, 3)]
     arrived([wo_sib])
-    arrived(a_moves)
-
-    lhs = attn[...].astype(F32).reshape(256, Q_COLS).astype(BF)
-    ring = [[], []]
-
-    def z_cols(p):
-        base = p * 768
-        return pl.ds(base, 768), pl.ds(base, 384), pl.ds(base + 384, 384)
-
-    def z_send(p, d):
-        cols, half0, half1 = z_cols(p)
-        if d == 4:
-            ring[p] = [
-                net.send(part.at[4, :, :, half1], zp_buf.at[3, :, :, half1], zdev[1]),
-                net.send(part.at[4, :, :, half0], zm_buf.at[3, :, :, half0], zdev[7]),
+    ring = {}
+
+    far0, far1 = slice(0, 768), slice(768, N_CHIP)
+
+    def project(*slots):
+        count = 64 * len(slots)
+        lhs = jnp.concatenate([attn[i].astype(F32).reshape(64, Q_COLS) for i in slots], 0).astype(BF)
+        for p in range(2):
+            cols = slice(p * 768, (p + 1) * 768)
+            block = jnp.dot(lhs, wo[:, cols], preferred_element_type=F32)
+            for k, i in enumerate(slots):
+                part[:, i, :, cols] = block[k * 64 : (k + 1) * 64].reshape(8, 8, 768).astype(BF)
+        for i in slots:
+            ring[i] = [
+                net.send(part.at[4, i, :, far1], zp_buf.at[3, i, :, far1], zdev[2]),
+                net.send(part.at[4, i, :, far0], zm_buf.at[3, i, :, far0], zdev[6]),
+                net.send(part.at[3, i], zp_buf.at[1, i], zdev[1]),
+                net.send(part.at[5, i], zm_buf.at[1, i], zdev[7]),
             ]
-        else:
-            ring[p] = [
-                net.send(part.at[d, :, :, cols], zp_buf.at[d - 1, :, :, cols], zdev[1]),
-                net.send(part.at[8 - d, :, :, cols], zm_buf.at[d - 1, :, :, cols], zdev[7]),
-            ]
-
-    def z_add(p, d):
-        cols, half0, half1 = z_cols(p)
-        arrived(ring[p])
-        if d == 3:
-            add_into(part.at[3, :, :, half1], zp_buf.at[3, :, :, half1])
-            add_into(part.at[5, :, :, half0], zm_buf.at[3, :, :, half0])
-        elif d > 0:
-            add_into(part.at[d, :, :, cols], zp_buf.at[d, :, :, cols])
-            add_into(part.at[8 - d, :, :, cols], zm_buf.at[d, :, :, cols])
-        else:
-            add_into(part.at[0, :, :, cols], zp_buf.at[0, :, :, cols], zm_buf.at[0, :, :, cols])
-
-    for p in range(2):
-        cols = slice(p * 768, (p + 1) * 768)
-        block = jnp.dot(lhs, wo[:, cols], preferred_element_type=F32).reshape(4, 8, 8, 768)
-        for i in range(4):
-            part[:, i, :, cols] = block[i].astype(BF)
-        z_send(p, 4)
-    for d in (3, 2, 1):
-        for p in range(2):
-            z_add(p, d)
-            z_send(p, d)
+
+    def relay(i):
+        arrived(ring[i])
+        add_into(part.at[2, i], zp_buf.at[1, i])
+        add_into(part.at[2, i, :, far1], zp_buf.at[3, i, :, far1])
+        add_into(part.at[6, i], zm_buf.at[1, i])
+        add_into(part.at[6, i, :, far0], zm_buf.at[3, i, :, far0])
+        ring[i] = [
+            net.send(part.at[2, i], zp_buf.at[2, i], zdev[2]),
+            net.send(part.at[6, i], zm_buf.at[2, i], zdev[6]),
+            net.send(part.at[1, i], zp_buf.at[0, i], zdev[1]),
+            net.send(part.at[7, i], zm_buf.at[0, i], zdev[7]),
+        ]
+
     p_moves = []
-    for p in range(2):
-        z_add(p, 0)
-        cols = z_cols(p)[0]
-        for d in (2, 1, 3):
-            p_moves.append(net.send(part.at[0, d, :, cols], px.at[4 - d, :, cols], xdev[d]))
+
+    def settle(i):
+        arrived(ring[i])
+        add_into(
+            part.at[0, i], zp_buf.at[0, i], zm_buf.at[0, i], zp_buf.at[2, i], zm_buf.at[2, i]
+        )
+        if i > 0:
+            p_moves.append(net.send(part.at[0, i], px.at[4 - i], xdev[i]))
+
+    project(0)
+    arrived([a_moves[1], a_moves[2]])
+    project(1, 3)
+    relay(0)
+    arrived([a_moves[0]])
+    project(2)
+    relay(1)
+    relay(3)
+    relay(2)
+    settle(0)
+    settle(1)
+    settle(3)
+    settle(2)
     px[0] = part[0, 0]
     load_res.wait()
     load_gain.wait()
@@ -580,17 +599,17 @@
             pltpu.VMEM((KEYS_CHIP + RESP, 2 * HEAD), BF),
             pltpu.VMEM((Q_COLS, N_CHIP), BF),
             pltpu.VMEM((4, 8, 8, Q_COLS), BF),
-            pltpu.VMEM((4, 2, 64, HEAD), F32),
+            pltpu.VMEM((4, 16, HEAD), F32),
             pltpu.VMEM((4, 8, 8, Q_COLS), BF),
-            pltpu.VMEM((4, 2, 64, HEAD), F32),
+            pltpu.VMEM((4, 16, HEAD), F32),
             pltpu.VMEM((4, 8, 8, Q_COLS), BF),
             pltpu.VMEM((8, 4, 8, N_CHIP), BF),
             pltpu.VMEM((4, 4, 8, N_CHIP), BF),
             pltpu.VMEM((4, 4, 8, N_CHIP), BF),
             pltpu.VMEM((4, 8, N_CHIP), BF),
             pltpu.SemaphoreType.DMA((10,)),
-            pltpu.SemaphoreType.DMA((64,)),
-            pltpu.SemaphoreType.DMA((64,)),
+            pltpu.SemaphoreType.DMA((72,)),
+            pltpu.SemaphoreType.DMA((72,)),
             pltpu.VMEM((8, 4, 8, D), BF),
             pltpu.VMEM((8, 4, 8, D), BF),
             pltpu.VMEM((256, hidden), F32),

time: 113 us -> 109 us (0.965)
  Pallas kernels: 111 us -> 106 us
    pallas_call x1, Pallas kernels: 111 us -> 106 us  [on_device(): pl.pallas_call(layer_kernel, name='layer', out_shape=jax.ShapeDtypeStruct...]
where the time goes in v5:
time: 109 us; the launch traced here: 108 us
  Pallas kernels  106 us (97%)
  local copies, waits for them, and re-layouts  1.54 us (1%)
    pallas_call x1, Pallas kernels, on_device(): pl.pallas_call(layer_kernel, name='layer', out_shape=jax.ShapeDtypeStruct...  106 us

profile of v5, /device:TPU:2, one launch (start us, length us, event | category | flops | bytes accessed | tf_op | source)
XLA Modules:
  0.0 107.6 jit_solution(1938559794989725621)
XLA Ops:
  0.0 106.1 %layer.1 = bf16[8,6144]{1,0:T(8,128)(2,1)} custom-call(bf16[8,6144]{1,0:T(8,128)(2,1)} %q_hbm.1, bf16[768,1024]{1,0:T(8,128)(2,1)} %ck_hbm.1, bf16[768,1024]{1,0:T(8,128)(2,1)} %cv_hbm.1, bf16[8,2048]{1,0:T(8,128)(2,1)} %rkv_hbm.1, s32[16,128]{1,0:T(8,128)} %bitcast.3, bf16[8,6144]{1,0:T(8,128)(2,1)} %res_hbm.1, bf16[192,768]{1,0:T(8,128)(2,1)} %wo_hbm.1, ...), custom_call_target="tpu_custom_call" | custom-call | tf_op jit(solution)/shard_map/layer/pallas_call | solution.py:577
  106.1 1.5 %copy.12 = bf16[8,6144]{1,0:T(8,128)(2,1)} copy(bf16[8,6144]{1,0:T(8,128)(2,1)} %layer.1) | data formatting | bytes 196608

commit v6 on v5

--- a/solution.py
+++ b/solution.py
@@ -21,7 +21,7 @@
 YI = {0: 0, 1: 1, -1: 2, 2: 3}
 ZGROUPS = (pl.ds(0, 1), pl.ds(1, 2), pl.ds(3, 2), pl.ds(5, 2), pl.ds(7, 1))
 
-A_COLS = 2560
+A_COLS = 2304
 B_COLS = D - A_COLS
 CA, A0, A1 = pl.ds(0, A_COLS), pl.ds(0, A_COLS // 2), pl.ds(A_COLS // 2, A_COLS // 2)
 CB = pl.ds(A_COLS, B_COLS)
@@ -80,15 +80,16 @@
 
 
 GATHER_ORDER = (
-    "ay1", "bz1", "by10", "az10", "ay2", "az11", "by11", "bz2", "by20", "az20", "az12", "az21",
-    "by21", "bz3", "az30", "by12", "az22", "az31", "bz4", "az40", "by13", "az32", "by22", "az41",
-    "by14", "az42", "up", "upb", "by23", "by24",
+    "ay1", "bz1", "by10", "ay2", "bz2", "az10", "az11", "by11", "az12", "by20", "bz3", "by12",
+    "bz4", "az20", "by21", "az21", "az22", "by13", "az30", "by22", "az31", "by14", "az32", "up",
+    "az40", "by23", "az41", "by24", "az42",
 )
 REDUCE_ORDER = (
-    "az42", "az41", "by04", "az40", "by03", "by02", "by01", "az32", "by00", "by14", "az31", "az30",
-    "az22", "by13", "bz4", "by12", "az21", "az20", "az12", "by11", "bz3", "by10", "az11", "ay0",
-    "az10", "bz2", "ay1", "bz1",
+    "az42", "by04", "az41", "az40", "by03", "by02", "az32", "by01", "az31", "by00", "az30", "by14",
+    "az22", "by13", "az21", "az20", "by12", "bz4", "az12", "bz3", "by11", "az11", "by10", "az10",
+    "ay0", "bz2", "ay1", "bz1",
 )
+BZ_NEEDS = {4: ("by14",), 3: ("by13",), 2: ("by12", "bz3", "bz4"), 1: ("by11",)}
 PIECES = (pl.ds(0, 1), pl.ds(1, 2), pl.ds(3, 1))
 
 
@@ -101,6 +102,7 @@
     x, core, z, y = where
     zp, zm = device(x, core, z + 1, y), device(x, core, z + 7, y)
     yp, ym = device(x, core, z, y + 1), device(x, core, z, y + 3)
+    zp2, zm2 = device(x, core, z + 2, y), device(x, core, z + 6, y)
 
     wide = mid_ref[...].astype(F32)
     mean = jnp.mean(wide, axis=-1, keepdims=True)
@@ -138,9 +140,23 @@
         flying["az%d%d" % (hop, piece)] = z_hop(hop, PIECES[piece], CA, A0, A1)
 
     def bz_hop(hop):
-        flying["bz%d" % hop] = z_hop(hop, 0, CB, B0, B1)
-
-    def up_cols(first, size, fresh, low=0, high=8):
+        if hop == 1:
+            pair = z_hop(1, 0, CB, B0, B1)
+        elif hop == 2:
+            pair = (
+                net.send(rows.at[0, 0, :, CB], rows.at[ZI[-2], 0, :, CB], zp2),
+                net.send(rows.at[0, 0, :, CB], rows.at[ZI[2], 0, :, CB], zm2),
+            )
+        elif hop == 3:
+            pair = z_hop(3, 0, CB, B0, B1)
+        else:
+            pair = (
+                net.send(rows.at[ZI[-2], 0, :, B0], rows.at[ZI[4], 0, :, B0], zp2),
+                net.send(rows.at[ZI[2], 0, :, B1], rows.at[ZI[4], 0, :, B1], zm2),
+            )
+        flying["bz%d" % hop] = pair
+
+    def up_cols(first, size, fresh, low, high):
         cols = pl.ds(first, size)
         count = (high - low) * 32
         block = rows[low:high, :, :, cols].astype(F32).reshape(count, size).astype(BF)
@@ -150,20 +166,22 @@
         else:
             acc[low * 32 : high * 32] += product
 
+    def up_rows(low, high):
+        for i in range(2):
+            up_cols(i * (A_COLS // 2), A_COLS // 2, i == 0, low, high)
+        for i in range(2):
+            up_cols(A_COLS + i * (B_COLS // 2), B_COLS // 2, False, low, high)
+
     own = pl.ds(0, 1)
     flying["ay1"] = y_first(own, CA)
     bz_hop(1)
+    bz_hop(2)
     flying["by10"] = y_first(ZGROUPS[0], CB)
     az_hop(1, 0)
     for name in GATHER_ORDER:
         if name == "up":
             load_up.wait()
-            for i in range(2):
-                up_cols(i * (A_COLS // 2), A_COLS // 2, i == 0)
-            continue
-        if name == "upb":
-            for i in range(2):
-                up_cols(A_COLS + i * (B_COLS // 2), B_COLS // 2, False, 0, 5)
+            up_rows(0, 5)
             continue
         for copy in flying[name]:
             copy.wait_recv()
@@ -176,14 +194,14 @@
         elif kind == "az" and step < 4:
             az_hop(step + 1, int(name[3]))
         elif kind == "bz":
-            if step < 4:
-                bz_hop(step + 1)
+            if step == 2:
+                bz_hop(3)
+                bz_hop(4)
             flying["by1%d" % step] = y_first(ZGROUPS[step], CB)
         elif kind == "by" and step == 1:
             flying["by2" + name[3]] = y_second(ZGROUPS[int(name[3])], B0, B1)
 
-    for i in range(2):
-        up_cols(A_COLS + i * (B_COLS // 2), B_COLS // 2, False, 5, 8)
+    up_rows(5, 8)
     up = jnp.maximum(acc[...], 0.0)
     act[...] = (up * up).astype(BF)
     load_down.wait()
@@ -240,7 +258,27 @@
             add_into(part.at[zs, 0, :, cols], got_p.at[0, zs, :, lcols], got_m.at[0, zs, :, lcols])
 
     za = [(p, CA, A0, A1, CA, A0, A1, a_zp, a_zm, p) for p in PIECES]
-    zb = (0, CB, B0, B1, LB, L0, L1, b_zp, b_zm, 0)
+
+    def bz_send(d):
+        slot, ahead, behind = {1: (0, zp, zm), 2: (2, zp2, zm2), 3: (1, zp, zm), 4: (3, zp2, zm2)}[d]
+        if d == 4:
+            return (
+                net.send(part.at[ZI[4], 0, :, B1], b_zp.at[slot, 0, :, L1], ahead),
+                net.send(part.at[ZI[4], 0, :, B0], b_zm.at[slot, 0, :, L0], behind),
+            )
+        return (
+            net.send(part.at[ZI[d], 0, :, CB], b_zp.at[slot, 0], ahead),
+            net.send(part.at[ZI[-d], 0, :, CB], b_zm.at[slot, 0], behind),
+        )
+
+    def bz_add(d):
+        if d == 4:
+            add_into(part.at[ZI[2], 0, :, B1], b_zp.at[3, 0, :, L1])
+            add_into(part.at[ZI[-2], 0, :, B0], b_zm.at[3, 0, :, L0])
+        elif d == 3:
+            add_into(part.at[ZI[2], 0, :, CB], b_zp.at[1, 0])
+            add_into(part.at[ZI[-2], 0, :, CB], b_zm.at[1, 0])
+
     yb = (CB, B0, B1, LB, L0, L1, b_yp, b_ym)
     ya = (CA, A0, A1, CA, A0, A1, a_yp, a_ym)
 
@@ -269,13 +307,13 @@
             flying["by1" + name[3]] = y_send(1, ZGROUPS[int(name[3])], *yb)
         elif kind == "by":
             y_add(1, ZGROUPS[int(name[3])], *yb)
-        elif kind == "bz" and step > 1:
-            z_add(step - 1, *zb)
+        elif kind == "bz":
+            bz_add(step)
         elif kind == "ay" and step == 0:
             y_add(0, own, *ya)
-        for d in (4, 3, 2, 1):
-            if "bz%d" % d not in flying and "by1%d" % d in done and (d == 4 or "bz%d" % (d + 1) in done):
-                flying["bz%d" % d] = z_send(d, *zb)
+        for d, needs in BZ_NEEDS.items():
+            if "bz%d" % d not in flying and done.issuperset(needs):
+                flying["bz%d" % d] = bz_send(d)
         if "ay1" not in flying and "ay0" in done and "az11" in done:
             flying["ay1"] = y_send(1, own, *ya)
         if name == "ay1":
@@ -291,6 +329,8 @@
                 + part[0, 0, :, CB].astype(F32)
                 + b_zp[0, 0].astype(F32)
                 + b_zm[0, 0].astype(F32)
+                + b_zp[2, 0].astype(F32)
+                + b_zm[2, 0].astype(F32)
             ).astype(BF)
     net.finish()
 

time: 109 us -> 106 us (0.972); the launches traced: 108 us -> 106 us
    pallas_call x1, Pallas kernels: 106 us -> 105 us  [on_device(): pl.pallas_call(layer_kernel, name='layer', out_shape=jax.ShapeDtypeStruct...]
where the time goes in v6:
time: 106 us
  Pallas kernels  105 us (99%)
  local copies, waits for them, and re-layouts  1.54 us (1%)
    pallas_call x1, Pallas kernels, on_device(): pl.pallas_call(layer_kernel, name='layer', out_shape=jax.ShapeDtypeStruct...  105 us

profile of v6, /device:TPU:2, one launch (start us, length us, event | category | flops | bytes accessed | tf_op | source)
XLA Modules:
  0.0 106.1 jit_solution(827494679444907308)
XLA Ops:
  0.0 104.6 %layer.1 = bf16[8,6144]{1,0:T(8,128)(2,1)} custom-call(bf16[8,6144]{1,0:T(8,128)(2,1)} %q_hbm.1, bf16[768,1024]{1,0:T(8,128)(2,1)} %ck_hbm.1, bf16[768,1024]{1,0:T(8,128)(2,1)} %cv_hbm.1, bf16[8,2048]{1,0:T(8,128)(2,1)} %rkv_hbm.1, s32[16,128]{1,0:T(8,128)} %bitcast.3, bf16[8,6144]{1,0:T(8,128)(2,1)} %res_hbm.1, bf16[192,768]{1,0:T(8,128)(2,1)} %wo_hbm.1, ...), custom_call_target="tpu_custom_call" | custom-call | tf_op jit(solution)/shard_map/layer/pallas_call | solution.py:617
  104.6 1.5 %copy.12 = bf16[8,6144]{1,0:T(8,128)(2,1)} copy(bf16[8,6144]{1,0:T(8,128)(2,1)} %layer.1) | data formatting | bytes 196608

commit v7 on v6

--- a/solution.py
+++ b/solution.py
@@ -35,6 +35,7 @@
     def __init__(self, send_sems, recv_sems):
         self.sems = send_sems, recv_sems
         self.made = []
+        self.finished = 0
 
     def send(self, src, dst, device):
         i = len(self.made)
@@ -50,9 +51,11 @@
         self.made.append(copy)
         return copy
 
-    def finish(self):
-        for copy in self.made:
+    def finish(self, but=0):
+        last = len(self.made) - but
+        for copy in self.made[self.finished : last]:
             copy.wait_send()
+        self.finished = max(self.finished, last)
 
 
 def where_am_i():
@@ -94,7 +97,7 @@
 
 
 def ffn_phase(
-    where, mid_ref, gain_ref, load_up, load_down, out_ref,
+    where, before, mid_ref, gain_ref, load_up, load_down, out_ref,
     up_w, down_w, rows, part, acc, act,
     a_zp, a_zm, a_yp, a_ym, b_yp, b_ym, b_zp, b_zm,
     g_send, g_recv, r_send, r_recv,
@@ -178,6 +181,7 @@
     bz_hop(2)
     flying["by10"] = y_first(ZGROUPS[0], CB)
     az_hop(1, 0)
+    before.finish()
     for name in GATHER_ORDER:
         if name == "up":
             load_up.wait()
@@ -211,7 +215,7 @@
         block = jnp.dot(act[...], down_w[:, cols], preferred_element_type=F32)
         part[:, :, :, cols] = block.reshape(8, 4, 8, size).astype(BF)
 
-    net.finish()
+    gather = net
     net = Copies(r_send, r_recv)
     flying = {}
     done = set()
@@ -290,6 +294,7 @@
         down_cols(A_COLS + i * (B_COLS // 2), B_COLS // 2)
     for g in (4, 3, 2, 1, 0):
         flying["by0%d" % g] = y_send(0, ZGROUPS[g], *yb)
+    gather.finish()
     for name in REDUCE_ORDER:
         for copy in flying[name]:
             copy.wait_recv()
@@ -314,6 +319,8 @@
         for d, needs in BZ_NEEDS.items():
             if "bz%d" % d not in flying and done.issuperset(needs):
                 flying["bz%d" % d] = bz_send(d)
+        if name in ("by14", "by12", "az10"):
+            net.finish(16)
         if "ay1" not in flying and "ay0" in done and "az11" in done:
             flying["ay1"] = y_send(1, own, *ya)
         if name == "ay1":
@@ -594,9 +601,8 @@
     for i in range(4):
         cols = pl.ds(pl.multiple_of(((x + i) & 3) * N_CHIP, HEAD), N_CHIP)
         mid_ref[:, cols] = (res_ref[:, cols].astype(F32) + px[i].astype(F32)).astype(BF)
-    net.finish()
     ffn_phase(
-        (x, core, z, y), mid_ref, gain_ref, load_up, load_down, out_ref, up_w, down_w, *ffn_refs
+        (x, core, z, y), net, mid_ref, gain_ref, load_up, load_down, out_ref, up_w, down_w, *ffn_refs
     )
 
 

time: 106 us -> 106 us (level)
  no operation moved by 1% of the time
where the time goes in v7:
time: 106 us
  Pallas kernels  104 us (98%)
  local copies, waits for them, and re-layouts  1.54 us (1%)
    pallas_call x1, Pallas kernels, on_device(): pl.pallas_call(layer_kernel, name='layer', out_shape=jax.ShapeDtypeStruct...  104 us

profile of v7, /device:TPU:2, one launch (start us, length us, event | category | flops | bytes accessed | tf_op | source)
XLA Modules:
  0.0 105.9 jit_solution(5986638806865035721)
XLA Ops:
  0.0 104.3 %layer.1 = bf16[8,6144]{1,0:T(8,128)(2,1)} custom-call(bf16[8,6144]{1,0:T(8,128)(2,1)} %q_hbm.1, bf16[768,1024]{1,0:T(8,128)(2,1)} %ck_hbm.1, bf16[768,1024]{1,0:T(8,128)(2,1)} %cv_hbm.1, bf16[8,2048]{1,0:T(8,128)(2,1)} %rkv_hbm.1, s32[16,128]{1,0:T(8,128)} %bitcast.3, bf16[8,6144]{1,0:T(8,128)(2,1)} %res_hbm.1, bf16[192,768]{1,0:T(8,128)(2,1)} %wo_hbm.1, ...), custom_call_target="tpu_custom_call" | custom-call | tf_op jit(solution)/shard_map/layer/pallas_call | solution.py:623
  104.3 1.5 %copy.12 = bf16[8,6144]{1,0:T(8,128)(2,1)} copy(bf16[8,6144]{1,0:T(8,128)(2,1)} %layer.1) | data formatting | bytes 196608

commit v8 on v7

--- a/solution.py
+++ b/solution.py
@@ -286,14 +286,24 @@
     yb = (CB, B0, B1, LB, L0, L1, b_yp, b_ym)
     ya = (CA, A0, A1, CA, A0, A1, a_yp, a_ym)
 
-    for i in range(2):
-        down_cols(i * (A_COLS // 2), A_COLS // 2)
+    down_cols(0, A_COLS // 2)
+    behind = {
+        p: net.send(part.at[ZI[4], PIECES[p], :, A0], a_zm.at[3, PIECES[p], :, A0], zm)
+        for p in (2, 1, 0)
+    }
+    down_cols(A_COLS // 2, A_COLS // 2)
     for p in (2, 1, 0):
-        flying["az4%d" % p] = z_send(4, *za[p])
-    for i in range(2):
-        down_cols(A_COLS + i * (B_COLS // 2), B_COLS // 2)
+        ahead = net.send(part.at[ZI[4], PIECES[p], :, A1], a_zp.at[3, PIECES[p], :, A1], zp)
+        flying["az4%d" % p] = ahead, behind[p]
+    down_cols(A_COLS, B_COLS // 2)
+    behind = {
+        g: net.send(part.at[ZGROUPS[g], YI[2], :, B0], b_ym.at[1, ZGROUPS[g], :, L0], ym)
+        for g in (4, 3, 2, 1, 0)
+    }
+    down_cols(A_COLS + B_COLS // 2, B_COLS // 2)
     for g in (4, 3, 2, 1, 0):
-        flying["by0%d" % g] = y_send(0, ZGROUPS[g], *yb)
+        ahead = net.send(part.at[ZGROUPS[g], YI[2], :, B1], b_yp.at[1, ZGROUPS[g], :, L1], yp)
+        flying["by0%d" % g] = ahead, behind[g]
     gather.finish()
     for name in REDUCE_ORDER:
         for copy in flying[name]:

time: 106 us -> 106 us (level)
  no operation moved by 1% of the time
where the time goes in v8:
time: 106 us
  Pallas kernels  104 us (98%)
  local copies, waits for them, and re-layouts  1.54 us (1%)
    pallas_call x1, Pallas kernels, on_device(): pl.pallas_call(layer_kernel, name='layer', out_shape=jax.ShapeDtypeStruct...  104 us

profile of v8, /device:TPU:2, one launch (start us, length us, event | category | flops | bytes accessed | tf_op | source)
XLA Modules:
  0.0 105.7 jit_solution(13819459243954554061)
XLA Ops:
  0.0 104.1 %layer.1 = bf16[8,6144]{1,0:T(8,128)(2,1)} custom-call(bf16[8,6144]{1,0:T(8,128)(2,1)} %q_hbm.1, bf16[768,1024]{1,0:T(8,128)(2,1)} %ck_hbm.1, bf16[768,1024]{1,0:T(8,128)(2,1)} %cv_hbm.1, bf16[8,2048]{1,0:T(8,128)(2,1)} %rkv_hbm.1, s32[16,128]{1,0:T(8,128)} %bitcast.3, bf16[8,6144]{1,0:T(8,128)(2,1)} %res_hbm.1, bf16[192,768]{1,0:T(8,128)(2,1)} %wo_hbm.1, ...), custom_call_target="tpu_custom_call" | custom-call | tf_op jit(solution)/shard_map/layer/pallas_call | solution.py:633
  104.2 1.5 %copy.12 = bf16[8,6144]{1,0:T(8,128)(2,1)} copy(bf16[8,6144]{1,0:T(8,128)(2,1)} %layer.1) | data formatting | bytes 196608
